TPU v7x, 128 devices: a whole 4x4x4 slice. The times are simulated.
128 devices in a mesh: row: 8 (over z_lo, x), col: 16 (over z_hi, y, core).
Axes of the slice: x: 4, y: 4, z: 4 (z_hi: 2, z_lo: 2; z = z_hi * 2 + z_lo), core: 2. Of those that a mesh axis runs over, the one named last changes fastest.
Arguments:
- stored: bfloat16 [16, 16, 12, 128, 128], P('row', 'col'), may hold values from -1.75 to 1.75
- block_cols: int32 [16, 16, 12], replicated, may hold values from 0 to 11, as said below
- out_cols: int32 [16, 16, 12, 8], P('row', 'col'), may hold values from 0 to 11, as said below
Outputs:
- window: bfloat16 [16, 16, 12, 8, 128, 128], P('row', 'col')
Inputs may be any that keep to these rules, and one draw needn't show every extreme that they name: Each block_cols[v, w, :] names every block column of its group exactly once. `out_cols`: every listed column receives at least one block product of the window; a column may be listed twice in one row.
All inputs are finite; a program needn't handle non-finite values.
Results may differ from a plain program's by a relative error of at most 0.001.
Values may be sent and summed in bfloat16 or wider, within the bound.
No kernel may reach another device: no remote copies, remote signals or barrier semaphores. Data moves between devices by JAX's collectives and lax.ppermute only.
A program may use at most 128 MiB of HBM per device.

v0:
```python
import functools

import jax
import jax.numpy as jnp
import numpy as np
from jax import lax
from jax.experimental import pallas as pl
from jax.experimental.pallas import tpu as pltpu
from jax.sharding import PartitionSpec as P

STEPS = 4
GRID = 16
ROWS = 8
COLS = 16
DEVICES = ROWS * COLS
AXES = ("row", "col")
TILE = 12
SIDE = 128
PIECE = 24
HOLDERS = 64

RIGHT_OWN, RIGHT_MIRROR, LEFT_OWN, LEFT_MIRROR = 0, 6, 12, 24
SLOTS = 36
CENTRE = (2, 3)
OUTER = (0, 1, 4, 5)


def slot_of(kind, rel, lead=0):
    return kind + (2 * rel + lead if kind in (LEFT_OWN, LEFT_MIRROR) else rel)


def centre_left(core):
    if core == 0:
        return ((LEFT_MIRROR, 3, 0), (LEFT_OWN, 3, 1), (LEFT_MIRROR, 3, 1), (LEFT_OWN, 2, 1))
    return ((LEFT_MIRROR, 2, 1), (LEFT_OWN, 2, 0), (LEFT_MIRROR, 2, 0), (LEFT_OWN, 3, 0))


def mirror_rels(core, high):
    return tuple(core + high + i for i in range(4))


def own_rels(core, high):
    rest = [rel for rel in mirror_rels(core, high) if rel not in CENTRE]
    return tuple(sorted(rest, key=lambda rel: rel % 2))


def shifted(tiles, by):
    return [(kind, rel + by, lead) for kind, rel, lead in tiles]


def from_neighbours(core):
    by = 2 * core * 2 - 2
    return shifted(centre_left(core)[:3], by), shifted(centre_left(1 - core)[1:], by)


def centre_slots(core, high):
    tiles = [(RIGHT_OWN, rel) for rel in CENTRE]
    tiles += [(RIGHT_MIRROR, rel) for rel in mirror_rels(core, high)]
    tiles += centre_left(core) + centre_left(1 - core)
    return [slot_of(*tile) for tile in tiles]


def outer_slots(core, high):
    tiles = [(RIGHT_OWN, rel) for rel in own_rels(core, high)]
    tiles += [(RIGHT_MIRROR, rel) for rel in mirror_rels(core, high)]
    missing = core if high else core + 4
    tiles += [(RIGHT_OWN, missing), (RIGHT_MIRROR, missing)]
    first, second = from_neighbours(core)
    tiles += first + second
    first, second = from_neighbours(1 - core)
    tiles += [first[0], second[2]]
    return [slot_of(*tile) for tile in tiles]


def slot_table(slots):
    return np.array([slots(core, high) for core in (0, 1) for high in (0, 1)], np.int32)


def source_of(tile, row, col):
    kind, rel, lead = tile
    ahead = (2 * row + 2 * (col // 2) + rel) % GRID
    own = 2 * row + lead
    lead, tail = {
        RIGHT_OWN: (ahead, col),
        RIGHT_MIRROR: (col, ahead),
        LEFT_OWN: (own, ahead),
        LEFT_MIRROR: (ahead, own),
    }[kind]
    return lead // 2 * COLS + tail, lead % 2


PAIRS = 5


def routes():
    table = np.zeros((2, DEVICES, PAIRS), np.int32)
    for device in range(DEVICES):
        row, col = divmod(device, COLS)
        core, high = col % 2, row % 2
        wanted = [[None] * PAIRS, [None] * PAIRS]
        for i in range(4):
            wanted[core][i] = (RIGHT_MIRROR, mirror_rels(core, high)[i], 0)
            wanted[1 - core][i] = centre_left(core)[i]
        for i in range(2):
            wanted[i][4] = (RIGHT_OWN, own_rels(core, high)[i], 0)
        for half in range(2):
            for pair in range(PAIRS):
                source, held = source_of(wanted[half][pair], row, col)
                assert held == half
                table[half, device, pair] = source
    return table


def pick_kernel(route_ref, held_ref, out_ref):
    group, pairs = out_ref.shape[:2]
    base = pl.program_id(0) * group * pairs

    def body(target, carry):
        for pair in range(pairs):
            out_ref[target, pair] = held_ref[route_ref[base + target * pairs + pair]]
        return carry

    lax.fori_loop(0, group, body, 0, unroll=4)


def pick(route, held):
    group = 16
    return pl.pallas_call(
        pick_kernel,
        grid_spec=pltpu.PrefetchScalarGridSpec(
            num_scalar_prefetch=1,
            grid=(DEVICES // group,),
            in_specs=[pl.BlockSpec((DEVICES, PIECE, SIDE), lambda t, *_: (0, 0, 0))],
            out_specs=pl.BlockSpec((group, PAIRS, PIECE, SIDE), lambda t, *_: (t, 0, 0, 0)),
        ),
        out_shape=jax.ShapeDtypeStruct((DEVICES, PAIRS, PIECE, SIDE), jnp.bfloat16),
        compiler_params=pltpu.CompilerParams(vmem_limit_bytes=16 << 20),
        cost_estimate=pl.CostEstimate(
            flops=0, bytes_accessed=2 * DEVICES * PAIRS * PIECE * SIDE * 2, transcendentals=0
        ),
    )(route, held)


def matmul(left, right, right_dim):
    return lax.dot_general(
        left, right, (((1,), (right_dim,)), ((), ())), preferred_element_type=jnp.float32
    )


def product_kernel(sources, last, cols_ref, kept_ref, place_ref, slot_ref, *refs):
    arrays, refs = refs[:sources], refs[sources:]
    if last:
        partial_ref, refs = refs[0], refs[1:]
    out_ref, tiles, total, right_inv, left_inv, sems = refs
    step = pl.program_id(0)
    slot, line = step // TILE, step % TILE
    row, col = place_ref[0], place_ref[1]
    core = col % 2
    first = 2 * row + col - core

    def group(rel):
        return (first + rel) % GRID

    def entry(lead, tail, line):
        return cols_ref[(lead * GRID + tail) * TILE + line]

    @pl.when(step == 0)
    def _():
        started = []
        for source in arrays:
            for position in range(source.shape[0]):
                index = len(started)
                started.append(
                    pltpu.make_async_copy(
                        source.at[position], tiles.at[slot_ref[index]], sems.at[index]
                    )
                )
        for copy in started:
            copy.start()
        for rel in OUTER if last else CENTRE:
            ahead = group(rel)
            for q in range(TILE):
                right_inv[rel * TILE + entry(col, ahead, q)] = q
                for half in range(2):
                    left_inv[(2 * rel + half) * TILE + entry(ahead, 2 * row + half, q)] = q
        for copy in started:
            copy.wait()

    total[...] = jnp.zeros_like(total)
    if last:
        edge = slot + core
        rels = (jnp.where(edge == 2, 4, edge), jnp.where(edge == 0, 1, 3 + edge))
    else:
        rels = CENTRE
    terms = []
    for rel in rels:
        ahead = group(rel)
        own_col = entry(2 * row + slot, ahead, line)
        mirror_col = left_inv[(2 * rel + slot) * TILE + line]
        own = tiles[LEFT_OWN + 2 * rel + slot, line]
        mirror = tiles[LEFT_MIRROR + 2 * rel + slot, mirror_col].T
        for left, middle in ((own, own_col), (mirror, mirror_col)):
            flipped = right_inv[rel * TILE + middle]
            terms.append(
                (entry(ahead, col, middle), matmul(left, tiles[RIGHT_OWN + rel, middle], 0))
            )
            terms.append((flipped, matmul(left, tiles[RIGHT_MIRROR + rel, flipped], 1)))
    for target, term in terms:
        total[target] += term
    kept_count = out_ref.shape[3]
    for o in range(kept_count):
        value = total[kept_ref[step * kept_count + o]]
        if last:
            value = value + partial_ref[0, 0, 0, o]
        out_ref[0, 0, 0, o] = value.astype(out_ref.dtype)


def products(cols, kept, place, slots, arrays, kept_count, partial=None):
    last = partial is not None
    copies = sum(a.shape[0] for a in arrays)
    block = pl.BlockSpec(
        (1, 1, 1, kept_count, SIDE, SIDE), lambda t, *_: (t // TILE, 0, t % TILE, 0, 0, 0)
    )
    dtype = jnp.bfloat16 if last else jnp.float32
    operands = list(arrays) + ([partial] if last else [])
    return pl.pallas_call(
        functools.partial(product_kernel, len(arrays), last),
        grid_spec=pltpu.PrefetchScalarGridSpec(
            num_scalar_prefetch=4,
            grid=(2 * TILE,),
            in_specs=[pl.BlockSpec(memory_space=pl.ANY)] * len(arrays) + [block] * last,
            out_specs=block,
            scratch_shapes=[
                pltpu.VMEM((SLOTS, TILE, SIDE, SIDE), jnp.bfloat16),
                pltpu.VMEM((TILE, SIDE, SIDE), jnp.float32),
                pltpu.SMEM((6 * TILE,), jnp.int32),
                pltpu.SMEM((12 * TILE,), jnp.int32),
                pltpu.SemaphoreType.DMA((copies,)),
            ],
        ),
        out_shape=jax.ShapeDtypeStruct((2, 1, TILE, kept_count, SIDE, SIDE), dtype),
        compiler_params=pltpu.CompilerParams(vmem_limit_bytes=28 << 20),
        cost_estimate=pl.CostEstimate(
            flops=192 * 2 * SIDE**3, bytes_accessed=25 << 20, transcendentals=0
        ),
    )(cols, kept, place, slots, *operands)


def moved(tiles, target):
    pairs = []
    for row in range(ROWS):
        for col in range(COLS):
            to_row, to_chip, to_core = target(row, col // 2, col % 2)
            to = to_row % ROWS * COLS + 2 * (to_chip % (COLS // 2)) + to_core
            pairs.append((row * COLS + col, to))
    return lax.ppermute(tiles, AXES, pairs)


def one(tiles, index):
    return lax.dynamic_slice_in_dim(tiles, index, 1, 0)


def on_device(stored, block_cols, out_cols):
    row, col = lax.axis_index("row"), lax.axis_index("col")
    core, high = col % 2, row % 2
    half = (row * COLS + col) // HOLDERS
    own_centre = moved(stored[:, 0], lambda r, m, c: (r - m - 1, m, c))
    spread = stored.reshape(DEVICES, PIECE, SIDE)
    held = lax.all_to_all(spread, AXES, split_axis=0, concat_axis=0, tiled=True)
    own_across = moved(one(own_centre, core), lambda r, m, c: (r ^ 1, m, c))
    route = jnp.asarray(routes().reshape(2, -1))[half]
    outgoing = pick(route, held)
    received = lax.all_to_all(outgoing, AXES, split_axis=0, concat_axis=0, tiled=True)
    received = received.reshape(2, HOLDERS, PAIRS, PIECE, SIDE)

    def gathered(pieces, count):
        return pieces[0, :, :count].transpose(1, 0, 2, 3).reshape(count, TILE, SIDE, SIDE)

    left = gathered(one(received, 1 - core), 4)
    forward = moved(left[:3], lambda r, m, c: (r, m + 1 - 2 * c, c))
    backward = moved(left[1:], lambda r, m, c: (r, m - 1 + 2 * c, 1 - c))
    sibling = moved(left, lambda r, m, c: (r, m, 1 - c))
    mirror = gathered(one(received, core), 4)
    mirror_across = moved(one(mirror, 2 - high), lambda r, m, c: (r ^ 1, m, c))
    own_outer = received[:, :, 4].reshape(2, TILE, SIDE, SIDE)
    shared = moved(
        jnp.concatenate([forward[:1], backward[2:]], 0), lambda r, m, c: (r, m, 1 - c)
    )
    which = 2 * core + high
    place = jnp.stack([row, col]).astype(jnp.int32)
    cols, kept = block_cols.reshape(-1), out_cols.reshape(-1)
    kept_count = out_cols.shape[3]
    partial = products(
        cols,
        kept,
        place,
        jnp.asarray(slot_table(centre_slots))[which],
        (own_centre, mirror, left, sibling),
        kept_count,
    )
    return products(
        cols,
        kept,
        place,
        jnp.asarray(slot_table(outer_slots))[which],
        (own_outer, mirror, own_across, mirror_across, forward, backward, shared),
        kept_count,
        partial,
    )


def solution(mesh):
    placed = (P("row", "col", None, None, None), P(), P("row", "col", None, None))
    return jax.shard_map(
        on_device,
        mesh=mesh,
        in_specs=placed,
        out_specs=P("row", "col", None, None, None, None),
        check_vma=False,
    )
```

profile of v0, /device:TPU:1, one launch (start us, length us, event | category | flops | bytes accessed | tf_op | source)
XLA Modules:
  0.0 186.5 jit_solution(5713282608954350295)
XLA Ops:
  0.0 11.5 %all-to-all-start = ((bf16[128,24,128]{2,1,0:T(8,128)(2,1)}), bf16[128,24,128]{2,1,0:T(8,128)(2,1)S(1)}, u32[]{:S(2)}, u32[]{:S(2)}) async-start(bf16[128,24,128]{2,1,0:T(8,128)(2,1)} %bitcast.3), calls=%async_computation | async-start | bytes 1572864 | tf_op jit(solution)/shard_map/all_to_all | solution.py:269
  11.6 16.1 %all-to-all-done.held_ref = bf16[128,24,128]{2,1,0:T(8,128)(2,1)S(1)} async-done(((bf16[128,24,128]{2,1,0:T(8,128)(2,1)}), bf16[128,24,128]{2,1,0:T(8,128)(2,1)S(1)}, u32[]{:S(2)}, u32[]{:S(2)}) %all-to-all-start) | async-done | bytes 786464 | tf_op jit(solution)/shard_map/all_to_all | solution.py:269
  27.7 1.7 shard_map.64
  29.4 1.9 %copy-done = bf16[128,5,24,128]{3,2,1,0:T(8,128)(2,1)} copy-done((bf16[128,5,24,128]{3,2,1,0:T(8,128)(2,1)}, bf16[128,5,24,128]{3,2,1,0:T(8,128)(2,1)S(1)}, u32[]{:S(2)}) %copy-start) | copy-done | bytes 3932184
  31.3 5.4 %all-to-all-start.1 = ((bf16[128,5,24,128]{3,2,1,0:T(8,128)(2,1)}), bf16[128,5,24,128]{3,2,1,0:T(8,128)(2,1)}, u32[]{:S(2)}, u32[]{:S(2)}) async-start(bf16[128,5,24,128]{3,2,1,0:T(8,128)(2,1)} %copy-done), calls=%async_computation.1 | async-start | bytes 7864320 | tf_op jit(solution)/shard_map/all_to_all | solution.py:273
  36.8 53.5 %all-to-all-done.1 = bf16[128,5,24,128]{3,2,1,0:T(8,128)(2,1)} async-done(((bf16[128,5,24,128]{3,2,1,0:T(8,128)(2,1)}), bf16[128,5,24,128]{3,2,1,0:T(8,128)(2,1)}, u32[]{:S(2)}, u32[]{:S(2)}) %all-to-all-start.1) | async-done | bytes 3932192 | tf_op jit(solution)/shard_map/all_to_all | solution.py:273
  90.3 3.6 %constant_dynamic-slice_fusion.1 = (bf16[1,64,4,24,128]{4,3,2,1,0:T(8,128)(2,1)S(1)}, bf16[1,64,4,24,128]{4,3,2,1,0:T(8,128)(2,1)}) fusion(bf16[2,64,5,24,128]{4,3,2,1,0:T(8,128)(2,1)} %bitcast.4, s32[]{:T(128)S(6)} %select_n.39, s32[]{:T(128)S(6)} %select_n.37), kind=kLoop, calls=%fused_computation.3 | loop fusion | bytes 6291464 | tf_op jit(solution)/shard_map/slice | solution.py:277
  93.8 0.3 copy.22
  94.1 0.3 fusion.3
  94.5 0.2 collective-permute-start.3
  94.7 0.0 collective-permute-start.4
  94.7 0.5 collective-permute-start.6
  95.2 5.7 %collective-permute-start = (bf16[2,12,128,128]{3,2,1,0:T(8,128)(2,1)}, bf16[2,12,128,128]{3,2,1,0:T(8,128)(2,1)S(1)}, u32[]{:S(2)}, u32[]{:S(2)}) collective-permute-start(bf16[2,12,128,128]{3,2,1,0:T(8,128)(2,1)} %bitcast.9), channel_id=1, source_target_pairs={{0,112},{1,113},{2,98},{3,99},{4,84},{5,85},{6,70},{7,71},{8,56},{... | collective-permute-start | bytes 2359304 | tf_op jit(solution)/shard_map/ppermute | solution.py:256
  100.9 21.0 %collective-permute-done.3.refs_4_ = bf16[3,12,128,128]{3,2,1,0:T(8,128)(2,1)S(1)} collective-permute-done((bf16[3,12,128,128]{3,2,1,0:T(8,128)(2,1)S(1)}, bf16[3,12,128,128]{3,2,1,0:T(8,128)(2,1)S(1)}, u32[]{:S(2)}, u32[]{:S(2)}) %collective-permute-start.3) | collective-permute-done | bytes 1179680 | tf_op jit(solution)/shard_map/ppermute | solution.py:256
  121.9 0.7 collective-permute-done.4.refs_5_
  122.6 1.0 copy-done.1
  123.6 1.0 pad_maximum_fusion
  124.6 20.2 %collective-permute-start.5 = (bf16[2,12,128,128]{3,2,1,0:T(8,128)(2,1)}, bf16[2,12,128,128]{3,2,1,0:T(8,128)(2,1)}, u32[]{:S(2)}, u32[]{:S(2)}) collective-permute-start(bf16[2,12,128,128]{3,2,1,0:T(8,128)(2,1)} %pad_maximum_fusion), channel_id=1, source_target_pairs={{0,1},{1,0},{2,3},{3,2},{4,5},{5,4},{6,7},{7,6},{8,9},{9,8},{10,11... | collective-permute-start | bytes 2359304 | tf_op jit(solution)/shard_map/ppermute | solution.py:256
  144.8 0.7 copy.11
  145.4 0.8 reshape.21.kept_ref
  146.3 1.7 copy.10
  147.9 1.0 reshape.20.cols_ref
  149.0 0.1 collective-permute-start.1
  149.1 1.7 copy.17
  150.9 1.5 collective-permute-start.2
  152.4 0.7 fusion.1.slot_ref
  153.1 0.7 fusion.slot_ref
  153.8 0.1 pad_add_fusion.place_ref
  153.8 1.2 slice.36
  155.1 12.8 %shard_map.65.refs_7_ = f32[2,1,12,8,128,128]{5,4,3,2,1,0:T(8,128)S(1)} custom-call(s32[3072]{0:T(1024)S(1)} %reshape.20.cols_ref, s32[192]{0:T(256)S(1)} %reshape.21.kept_ref, s32[2]{0:T(128)S(1)} %pad_add_fusion.place_ref, s32[14]{0:T(128)S(1)} %fusion.1.slot_ref, bf16[2,12,128,128]{3,2,1,0:T(8,128)(2,1)S(1)} %collective-permute-done.refs_0_, ...), custom_call_target="tpu_custom_call" | custom-call | flops 805306368 | bytes 26214400 | tf_op jit(solution)/shard_map/pallas_call | solution.py:226
  167.9 0.4 collective-permute-done.2.refs_3_
  168.3 18.2 %shard_map.66 = bf16[2,1,12,8,128,128]{5,4,3,2,1,0:T(8,128)(2,1)} custom-call(s32[3072]{0:T(1024)S(1)} %reshape.20.cols_ref, s32[192]{0:T(256)S(1)} %reshape.21.kept_ref, s32[2]{0:T(128)S(1)} %pad_add_fusion.place_ref, s32[16]{0:T(128)S(1)} %fusion.slot_ref, bf16[2,12,128,128]{3,2,1,0:T(8,128)(2,1)S(1)} %bitcast.33, bf16[4,12,128,128]{3,2,1,0:T(8,128)(2,1)S(1)} %bitcast.32, ...), custom_call_target="tpu_custom_call" | custom-call | flops 805306368 | bytes 26214400 | tf_op jit(solution)/shard_map/pallas_call | solution.py:226
  (17 shorter events, 0.2 us)
Async XLA Ops:
  0.0 11.5 %copy-start.4 = (s32[2,640]{1,0:T(2,128)S(1)}, s32[2,640]{1,0:T(2,128)}, u32[]{:S(2)}) copy-start(s32[2,640]{1,0:T(2,128)} %constant.55.clone) | copy-start | bytes 15364
  0.0 27.7 %all-to-all-start = ((bf16[128,24,128]{2,1,0:T(8,128)(2,1)}), bf16[128,24,128]{2,1,0:T(8,128)(2,1)S(1)}, u32[]{:S(2)}, u32[]{:S(2)}) async-start(bf16[128,24,128]{2,1,0:T(8,128)(2,1)} %bitcast.3), calls=%async_computation | async-start | bytes 1572864 | tf_op jit(solution)/shard_map/all_to_all | solution.py:269
  29.4 1.9 %copy-start = (bf16[128,5,24,128]{3,2,1,0:T(8,128)(2,1)}, bf16[128,5,24,128]{3,2,1,0:T(8,128)(2,1)S(1)}, u32[]{:S(2)}) copy-start(bf16[128,5,24,128]{3,2,1,0:T(8,128)(2,1)S(1)} %shard_map.64) | copy-start | bytes 11796484
  31.3 59.0 %all-to-all-start.1 = ((bf16[128,5,24,128]{3,2,1,0:T(8,128)(2,1)}), bf16[128,5,24,128]{3,2,1,0:T(8,128)(2,1)}, u32[]{:S(2)}, u32[]{:S(2)}) async-start(bf16[128,5,24,128]{3,2,1,0:T(8,128)(2,1)} %copy-done), calls=%async_computation.1 | async-start | bytes 7864320 | tf_op jit(solution)/shard_map/all_to_all | solution.py:273
  94.5 27.4 %collective-permute-start.3 = (bf16[3,12,128,128]{3,2,1,0:T(8,128)(2,1)S(1)}, bf16[3,12,128,128]{3,2,1,0:T(8,128)(2,1)S(1)}, u32[]{:S(2)}, u32[]{:S(2)}) collective-permute-start(bf16[3,12,128,128]{3,2,1,0:T(8,128)(2,1)S(1)} %bitcast.35), channel_id=1, source_target_pairs={{0,2},{1,15},{2,4},{3,1},{4,6},{5,3},{6,8},{7,5},{8,10},{9,7},{10,... | collective-permute-start | bytes 3538952 | tf_op jit(solution)/shard_map/ppermute | solution.py:256
  94.7 27.8 %collective-permute-start.4 = (bf16[3,12,128,128]{3,2,1,0:T(8,128)(2,1)S(1)}, bf16[3,12,128,128]{3,2,1,0:T(8,128)(2,1)S(1)}, u32[]{:S(2)}, u32[]{:S(2)}) collective-permute-start(bf16[3,12,128,128]{3,2,1,0:T(8,128)(2,1)S(1)} %bitcast.34), channel_id=1, source_target_pairs={{0,15},{1,2},{2,1},{3,4},{4,3},{5,6},{6,5},{7,8},{8,7},{9,10},{10,... | collective-permute-start | bytes 3538952 | tf_op jit(solution)/shard_map/ppermute | solution.py:256
  94.7 60.4 %collective-permute-start.6 = (bf16[4,12,128,128]{3,2,1,0:T(8,128)(2,1)S(1)}, bf16[4,12,128,128]{3,2,1,0:T(8,128)(2,1)}, u32[]{:S(2)}, u32[]{:S(2)}) collective-permute-start(bf16[4,12,128,128]{3,2,1,0:T(8,128)(2,1)S(1)} %bitcast.28), channel_id=1, source_target_pairs={{0,1},{1,0},{2,3},{3,2},{4,5},{5,4},{6,7},{7,6},{8,9},{9,8},{10,11... | collective-permute-start | bytes 4718600 | tf_op jit(solution)/shard_map/ppermute | solution.py:256
  95.2 49.6 %copy-start.3 = (s32[2,1,12,8]{2,3,1,0:T(8,128)S(1)}, s32[2,1,12,8]{2,3,1,0:T(8,128)}, u32[]{:S(2)}) copy-start(s32[2,1,12,8]{2,3,1,0:T(8,128)} %param.8) | copy-start | bytes 2308
  95.2 53.8 %collective-permute-start = (bf16[2,12,128,128]{3,2,1,0:T(8,128)(2,1)}, bf16[2,12,128,128]{3,2,1,0:T(8,128)(2,1)S(1)}, u32[]{:S(2)}, u32[]{:S(2)}) collective-permute-start(bf16[2,12,128,128]{3,2,1,0:T(8,128)(2,1)} %bitcast.9), channel_id=1, source_target_pairs={{0,112},{1,113},{2,98},{3,99},{4,84},{5,85},{6,70},{7,71},{8,56},{... | collective-permute-start | bytes 2359304 | tf_op jit(solution)/shard_map/ppermute | solution.py:256
  122.6 1.0 copy-start.1
  124.6 43.7 %collective-permute-start.5 = (bf16[2,12,128,128]{3,2,1,0:T(8,128)(2,1)}, bf16[2,12,128,128]{3,2,1,0:T(8,128)(2,1)}, u32[]{:S(2)}, u32[]{:S(2)}) collective-permute-start(bf16[2,12,128,128]{3,2,1,0:T(8,128)(2,1)} %pad_maximum_fusion), channel_id=1, source_target_pairs={{0,1},{1,0},{2,3},{3,2},{4,5},{5,4},{6,7},{7,6},{8,9},{9,8},{10,11... | collective-permute-start | bytes 2359304 | tf_op jit(solution)/shard_map/ppermute | solution.py:256
  149.0 18.8 %collective-permute-start.1 = (bf16[1,12,128,128]{3,2,1,0:T(8,128)(2,1)S(1)}, bf16[1,12,128,128]{3,2,1,0:T(8,128)(2,1)S(1)}, u32[]{:S(2)}, u32[]{:S(2)}) collective-permute-start(bf16[1,12,128,128]{3,2,1,0:T(8,128)(2,1)S(1)} %constant_dynamic-slice_fusion.3), channel_id=1, source_target_pairs={{0,16},{1,17},{2,18},{3,19},{4,20},{5,21},{6,22},{7,23},{8,24},{9,... | collective-permute-start | bytes 1179656 | tf_op jit(solution)/shard_map/ppermute | solution.py:256
  150.9 17.4 %collective-permute-start.2 = (bf16[1,12,128,128]{3,2,1,0:T(8,128)(2,1)S(1)}, bf16[1,12,128,128]{3,2,1,0:T(8,128)(2,1)S(1)}, u32[]{:S(2)}, u32[]{:S(2)}) collective-permute-start(bf16[1,12,128,128]{3,2,1,0:T(8,128)(2,1)S(1)} %constant_dynamic-slice_fusion.2), channel_id=1, source_target_pairs={{0,16},{1,17},{2,18},{3,19},{4,20},{5,21},{6,22},{7,23},{8,24},{9,... | collective-permute-start | bytes 1179656 | tf_op jit(solution)/shard_map/ppermute | solution.py:256
  155.1 13.2 %copy-start.2 = (bf16[3,12,128,128]{3,2,1,0:T(8,128)(2,1)S(1)}, bf16[3,12,128,128]{3,2,1,0:T(8,128)(2,1)}, u32[]{:S(2)}) copy-start(bf16[3,12,128,128]{3,2,1,0:T(8,128)(2,1)} %copy-done.1) | copy-start | bytes 3538948
where the time goes:
time: 187 us; the launch traced here: 186 us
  waiting for transfers between devices  91.7 us (49%)
  starting transfers between devices  45.1 us (24%)
  Pallas kernels  32.6 us (17%)
  local copies, waits for them, and re-layouts  15.8 us (8%)
    all_to_all x1, waiting for transfers between devices, on_device(): lax.all_to_all(outgoing, AXES, split_axis=0, concat_axis=0, tiled=True)  53.5 us
    pallas_call x2, Pallas kernels, products(): pl.pallas_call(functools.partial(product_kernel, len(arrays), last), grid...  30.9 us
    ppermute x7, starting transfers between devices, moved(): return lax.ppermute(tiles, AXES, pairs)  28.2 us
    ppermute x7, waiting for transfers between devices, moved(): return lax.ppermute(tiles, AXES, pairs)  22.1 us
    all_to_all x1, waiting for transfers between devices, on_device(): held = lax.all_to_all(spread, AXES, split_axis=0, concat_axis=0, tiled=True)  16.1 us
    all_to_all x1, starting transfers between devices, on_device(): held = lax.all_to_all(spread, AXES, split_axis=0, concat_axis=0, tiled=True)  11.5 us
    unnamed x14, local copies, waits for them, and re-layouts  7.3 us
    all_to_all x1, starting transfers between devices, on_device(): lax.all_to_all(outgoing, AXES, split_axis=0, concat_axis=0, tiled=True)  5.44 us
  transfers between devices with their start and end apart: 9, of which 5 were waited for; matrix products, arithmetic and copies ran while one was open for 5% of the time, Pallas kernels for 7%

commit v1 on v0

v1 whole, which is shorter than its diff:
```python
import functools

import jax
import jax.numpy as jnp
import numpy as np
from jax import lax
from jax.experimental import pallas as pl
from jax.experimental.pallas import tpu as pltpu
from jax.sharding import PartitionSpec as P

STEPS = 4
GRID = 16
ROWS = 8
COLS = 16
DEVICES = ROWS * COLS
AXES = ("row", "col")
TILE = 12
SIDE = 128
PIECE = 24
HOLDERS = 64

RIGHT_OWN, RIGHT_MIRROR, LEFT_OWN, LEFT_MIRROR = 0, 6, 12, 24
SLOTS = 36
CENTRE = (2, 3)
OUTER = (0, 1, 4, 5)


def slot_of(kind, rel, lead=0):
    return kind + (2 * rel + lead if kind in (LEFT_OWN, LEFT_MIRROR) else rel)


def centre_left(core):
    if core == 0:
        return ((LEFT_MIRROR, 3, 0), (LEFT_OWN, 3, 1), (LEFT_MIRROR, 3, 1), (LEFT_OWN, 2, 1))
    return ((LEFT_MIRROR, 2, 1), (LEFT_OWN, 2, 0), (LEFT_MIRROR, 2, 0), (LEFT_OWN, 3, 0))


def mirror_rels(core, high):
    return tuple(core + high + i for i in range(4))


def own_rels(core, high):
    rels = mirror_rels(core, high)
    return tuple(sorted(rels[:2], key=lambda rel: rel % 2)) + tuple(
        sorted(rels[2:], key=lambda rel: rel % 2)
    )


def shifted(tiles, by):
    return [(kind, rel + by, lead) for kind, rel, lead in tiles]


def from_neighbours(core):
    by = 2 * core * 2 - 2
    return shifted(centre_left(core)[:3], by), shifted(centre_left(1 - core)[1:], by)


def rights(array, kind, held, wanted):
    return [(array, held.index(rel), slot_of(kind, rel)) for rel in held if rel in wanted]


def centre_copies(core, high):
    copies = rights(0, RIGHT_OWN, own_rels(core, high), CENTRE)
    copies += rights(1, RIGHT_MIRROR, mirror_rels(core, high), CENTRE)
    copies += [(2, i, slot_of(*tile)) for i, tile in enumerate(centre_left(core))]
    copies += [(3, i, slot_of(*tile)) for i, tile in enumerate(centre_left(1 - core))]
    return copies


def outer_copies(core, high):
    copies = rights(0, RIGHT_OWN, own_rels(core, high), OUTER)
    copies += rights(1, RIGHT_MIRROR, mirror_rels(core, high), OUTER)
    missing = core if high else core + 4
    copies += [(2, 0, slot_of(RIGHT_OWN, missing)), (2, 1, slot_of(RIGHT_MIRROR, missing))]
    first, second = from_neighbours(core)
    copies += [(3, i, slot_of(*tile)) for i, tile in enumerate(first)]
    copies += [(4, i, slot_of(*tile)) for i, tile in enumerate(second)]
    first, second = from_neighbours(1 - core)
    copies += [(5, 0, slot_of(*first[0])), (5, 1, slot_of(*second[2]))]
    return copies


def copy_arrays(copies):
    return tuple(array for array, _, _ in copies(0, 0))


def copy_table(copies):
    table = []
    for core in (0, 1):
        for high in (0, 1):
            listed = copies(core, high)
            assert tuple(c[0] for c in listed) == copy_arrays(copies)
            table.append([c[1] for c in listed] + [c[2] for c in listed])
    return np.array(table, np.int32)


def source_of(tile, row, col):
    kind, rel, lead = tile
    ahead = (2 * row + 2 * (col // 2) + rel) % GRID
    own = 2 * row + lead
    lead, tail = {
        RIGHT_OWN: (ahead, col),
        RIGHT_MIRROR: (col, ahead),
        LEFT_OWN: (own, ahead),
        LEFT_MIRROR: (ahead, own),
    }[kind]
    return lead // 2 * COLS + tail, lead % 2


PAIRS = 6


def routes():
    table = np.zeros((2, DEVICES, PAIRS), np.int32)
    for device in range(DEVICES):
        row, col = divmod(device, COLS)
        core, high = col % 2, row % 2
        wanted = [[None] * PAIRS, [None] * PAIRS]
        for i in range(4):
            wanted[core][i] = (RIGHT_MIRROR, mirror_rels(core, high)[i], 0)
            wanted[1 - core][i] = centre_left(core)[i]
            wanted[i % 2][4 + i // 2] = (RIGHT_OWN, own_rels(core, high)[i], 0)
        for half in range(2):
            for pair in range(PAIRS):
                source, held = source_of(wanted[half][pair], row, col)
                assert held == half
                table[half, device, pair] = source
    return table


def pick_kernel(route_ref, held_ref, out_ref):
    group, pairs = out_ref.shape[:2]
    base = pl.program_id(0) * group * pairs

    def body(target, carry):
        for pair in range(pairs):
            out_ref[target, pair] = held_ref[route_ref[base + target * pairs + pair]]
        return carry

    lax.fori_loop(0, group, body, 0, unroll=4)


def pick(route, held):
    group = 16
    return pl.pallas_call(
        pick_kernel,
        grid_spec=pltpu.PrefetchScalarGridSpec(
            num_scalar_prefetch=1,
            grid=(DEVICES // group,),
            in_specs=[pl.BlockSpec((DEVICES, PIECE, SIDE), lambda t, *_: (0, 0, 0))],
            out_specs=pl.BlockSpec((group, PAIRS, PIECE, SIDE), lambda t, *_: (t, 0, 0, 0)),
        ),
        out_shape=jax.ShapeDtypeStruct((DEVICES, PAIRS, PIECE, SIDE), jnp.bfloat16),
        compiler_params=pltpu.CompilerParams(vmem_limit_bytes=16 << 20),
        cost_estimate=pl.CostEstimate(
            flops=0, bytes_accessed=2 * DEVICES * PAIRS * PIECE * SIDE * 2, transcendentals=0
        ),
    )(route, held)


def matmul(left, right, right_dim):
    return lax.dot_general(
        left, right, (((1,), (right_dim,)), ((), ())), preferred_element_type=jnp.float32
    )


def product_kernel(sources, from_arrays, last, cols_ref, kept_ref, place_ref, copy_ref, *refs):
    arrays, refs = refs[:sources], refs[sources:]
    if last:
        partial_ref, refs = refs[0], refs[1:]
    out_ref, tiles, total, right_inv, left_inv, sems = refs
    lines, kept_count = out_ref.shape[2:4]
    step = pl.program_id(0)
    slot = step * lines // TILE
    row, col = place_ref[0], place_ref[1]
    core = col % 2
    first = 2 * row + col - core

    def group(rel):
        return (first + rel) % GRID

    def entry(lead, tail, line):
        return cols_ref[(lead * GRID + tail) * TILE + line]

    @pl.when(step == 0)
    def _():
        count = len(from_arrays)
        started = [
            pltpu.make_async_copy(
                arrays[array].at[copy_ref[index]],
                tiles.at[copy_ref[count + index]],
                sems.at[index],
            )
            for index, array in enumerate(from_arrays)
        ]
        for copy in started:
            copy.start()
        for rel in OUTER if last else CENTRE:
            ahead = group(rel)
            for q in range(TILE):
                right_inv[rel * TILE + entry(col, ahead, q)] = q
                for half in range(2):
                    left_inv[(2 * rel + half) * TILE + entry(ahead, 2 * row + half, q)] = q
        for copy in started:
            copy.wait()

    total[...] = jnp.zeros_like(total)
    if last:
        edge = slot + core
        rels = (jnp.where(edge == 2, 4, edge), jnp.where(edge == 0, 1, 3 + edge))
    else:
        rels = CENTRE
    terms = []
    for sub in range(lines):
        line = step * lines % TILE + sub
        for rel in rels:
            ahead = group(rel)
            own_col = entry(2 * row + slot, ahead, line)
            mirror_col = left_inv[(2 * rel + slot) * TILE + line]
            own = tiles[LEFT_OWN + 2 * rel + slot, line]
            mirror = tiles[LEFT_MIRROR + 2 * rel + slot, mirror_col].T
            for left, middle in ((own, own_col), (mirror, mirror_col)):
                flipped = right_inv[rel * TILE + middle]
                straight = matmul(left, tiles[RIGHT_OWN + rel, middle], 0)
                terms.append((sub, entry(ahead, col, middle), straight))
                terms.append((sub, flipped, matmul(left, tiles[RIGHT_MIRROR + rel, flipped], 1)))
    for sub, target, term in terms:
        total[sub, target] += term
    for sub in range(lines):
        for o in range(kept_count):
            value = total[sub, kept_ref[(step * lines + sub) * kept_count + o]]
            if last:
                value = value + partial_ref[0, 0, sub, o]
            out_ref[0, 0, sub, o] = value.astype(out_ref.dtype)


def products(cols, kept, place, table, arrays, from_arrays, kept_count, partial=None):
    last = partial is not None
    lines = 2
    block = pl.BlockSpec(
        (1, 1, lines, kept_count, SIDE, SIDE),
        lambda t, *_: (t * lines // TILE, 0, t % (TILE // lines), 0, 0, 0),
    )
    dtype = jnp.bfloat16 if last else jnp.float32
    operands = list(arrays) + ([partial] if last else [])
    return pl.pallas_call(
        functools.partial(product_kernel, len(arrays), from_arrays, last),
        grid_spec=pltpu.PrefetchScalarGridSpec(
            num_scalar_prefetch=4,
            grid=(2 * TILE // lines,),
            in_specs=[pl.BlockSpec(memory_space=pl.ANY)] * len(arrays) + [block] * last,
            out_specs=block,
            scratch_shapes=[
                pltpu.VMEM((SLOTS, TILE, SIDE, SIDE), jnp.bfloat16),
                pltpu.VMEM((lines, TILE, SIDE, SIDE), jnp.float32),
                pltpu.SMEM((6 * TILE,), jnp.int32),
                pltpu.SMEM((12 * TILE,), jnp.int32),
                pltpu.SemaphoreType.DMA((len(from_arrays),)),
            ],
        ),
        out_shape=jax.ShapeDtypeStruct((2, 1, TILE, kept_count, SIDE, SIDE), dtype),
        compiler_params=pltpu.CompilerParams(vmem_limit_bytes=30 << 20),
        cost_estimate=pl.CostEstimate(
            flops=192 * 2 * SIDE**3, bytes_accessed=25 << 20, transcendentals=0
        ),
    )(cols, kept, place, table, *operands)


def moved(tiles, target):
    pairs = []
    for row in range(ROWS):
        for col in range(COLS):
            to_row, to_chip, to_core = target(row, col // 2, col % 2)
            to = to_row % ROWS * COLS + 2 * (to_chip % (COLS // 2)) + to_core
            pairs.append((row * COLS + col, to))
    return lax.ppermute(tiles, AXES, pairs)


def one(tiles, index):
    return lax.dynamic_slice_in_dim(tiles, index, 1, 0)


def on_device(stored, block_cols, out_cols):
    row, col = lax.axis_index("row"), lax.axis_index("col")
    core, high = col % 2, row % 2
    half = (row * COLS + col) // HOLDERS
    which = 2 * core + high
    spread = stored.reshape(DEVICES, PIECE, SIDE)
    held = lax.all_to_all(spread, AXES, split_axis=0, concat_axis=0, tiled=True)
    scalars = (
        block_cols.reshape(-1),
        out_cols.reshape(-1),
        jnp.stack([row, col]).astype(jnp.int32),
        jnp.asarray(copy_table(centre_copies))[which],
        jnp.asarray(copy_table(outer_copies))[which],
    )
    held, scalars = lax.optimization_barrier((held, scalars))
    cols, kept, place, centre, outer = scalars
    route = jnp.asarray(routes().reshape(2, -1))[half]
    outgoing = pick(route, held)
    received = lax.all_to_all(outgoing, AXES, split_axis=0, concat_axis=0, tiled=True)
    received = received.reshape(2, HOLDERS, PAIRS, PIECE, SIDE)

    def gathered(pieces, start, count):
        pieces = pieces[:, :, start : start + count].transpose(2, 0, 1, 3, 4)
        return pieces.reshape(-1, TILE, SIDE, SIDE)

    left = gathered(one(received, 1 - core), 0, 4)
    forward = moved(left[:3], lambda r, m, c: (r, m + 1 - 2 * c, c))
    backward = moved(left[1:], lambda r, m, c: (r, m - 1 + 2 * c, 1 - c))
    sibling = moved(left, lambda r, m, c: (r, m, 1 - c))
    mirror = gathered(one(received, core), 0, 4)
    own = gathered(received, 4, 2)
    sent = jnp.concatenate([one(own, 2 * (1 - high) + core), one(mirror, 2 - high)], 0)
    across = moved(sent, lambda r, m, c: (r ^ 1, m, c))
    kept_count = out_cols.shape[3]
    partial = products(
        cols,
        kept,
        place,
        centre,
        (own, mirror, left, sibling),
        copy_arrays(centre_copies),
        kept_count,
    )
    forward, backward, across, partial = lax.optimization_barrier(
        (forward, backward, across, partial)
    )
    shared = moved(
        jnp.concatenate([forward[:1], backward[2:]], 0), lambda r, m, c: (r, m, 1 - c)
    )
    return products(
        cols,
        kept,
        place,
        outer,
        (own, mirror, across, forward, backward, shared),
        copy_arrays(outer_copies),
        kept_count,
        partial,
    )


def solution(mesh):
    placed = (P("row", "col", None, None, None), P(), P("row", "col", None, None))
    return jax.shard_map(
        on_device,
        mesh=mesh,
        in_specs=placed,
        out_specs=P("row", "col", None, None, None, None),
        check_vma=False,
    )
```

time: 187 us -> 154 us (0.82)
  starting transfers between devices: 45.1 us -> 22.5 us
  Pallas kernels: 32.6 us -> 23.7 us
    ppermute x7 -> x5, starting transfers between devices: 28.2 us -> 5.56 us  [moved(): return lax.ppermute(tiles, AXES, pairs)]
    pallas_call x2, Pallas kernels: 30.9 us -> 22 us  [products(): pl.pallas_call(functools.partial(product_kernel, len(arrays), from_arrays...]
    all_to_all x1, waiting for transfers between devices: 53.5 us -> 62.3 us  [on_device(): lax.all_to_all(outgoing, AXES, split_axis=0, concat_axis=0, tiled=True)]
    ppermute x7 -> x5, waiting for transfers between devices: 22.1 us -> 15.8 us  [moved(): return lax.ppermute(tiles, AXES, pairs)]
    unnamed x14 -> x15, local copies, waits for them, and re-layouts: 7.3 us -> 4.39 us
    all_to_all x1, waiting for transfers between devices: 16.1 us -> 14.2 us  [on_device(): held = lax.all_to_all(spread, AXES, split_axis=0, concat_axis=0, tiled=True)]
  transfers between devices with their start and end apart: 9 -> 7, of which waited for: 5 -> 6; matrix products, arithmetic and copies ran while one was open for 5% -> 4% of each run, Pallas kernels for 7% -> 6%
where the time goes in v1:
time: 154 us; the launch traced here: 153 us
  waiting for transfers between devices  92.3 us (60%)
  Pallas kernels  23.7 us (15%)
  starting transfers between devices  22.5 us (15%)
  local copies, waits for them, and re-layouts  14.2 us (9%)
    all_to_all x1, waiting for transfers between devices, on_device(): lax.all_to_all(outgoing, AXES, split_axis=0, concat_axis=0, tiled=True)  62.3 us
    pallas_call x2, Pallas kernels, products(): pl.pallas_call(functools.partial(product_kernel, len(arrays), from_arrays...  22 us
    ppermute x5, waiting for transfers between devices, moved(): return lax.ppermute(tiles, AXES, pairs)  15.8 us
    all_to_all x1, waiting for transfers between devices, on_device(): held = lax.all_to_all(spread, AXES, split_axis=0, concat_axis=0, tiled=True)  14.2 us
    all_to_all x1, starting transfers between devices, on_device(): held = lax.all_to_all(spread, AXES, split_axis=0, concat_axis=0, tiled=True)  11.5 us
    ppermute x5, starting transfers between devices, moved(): return lax.ppermute(tiles, AXES, pairs)  5.56 us
    all_to_all x1, starting transfers between devices, on_device(): lax.all_to_all(outgoing, AXES, split_axis=0, concat_axis=0, tiled=True)  5.47 us
    slice x2, local copies, waits for them, and re-layouts, gathered(): pieces = pieces[:, :, start:start + count].transpose(2, 0, 1, 3, 4)  5.27 us
  transfers between devices with their start and end apart: 7, of which 6 were waited for; matrix products, arithmetic and copies ran while one was open for 4% of the time, Pallas kernels for 6%

profile of v1, /device:TPU:1, one launch (start us, length us, event | category | flops | bytes accessed | tf_op | source)
XLA Modules:
  0.0 153.2 jit_solution(2888134680478370772)
XLA Ops:
  0.0 11.5 %all-to-all-start = ((bf16[128,24,128]{2,1,0:T(8,128)(2,1)}), bf16[128,24,128]{2,1,0:T(8,128)(2,1)S(1)}, u32[]{:S(2)}, u32[]{:S(2)}) async-start(bf16[128,24,128]{2,1,0:T(8,128)(2,1)} %bitcast.31), calls=%async_computation | async-start | bytes 1572864 | tf_op jit(solution)/shard_map/all_to_all | solution.py:289
  11.6 0.1 copy.11
  11.7 0.1 reshape.25.kept_ref
  11.8 0.2 copy.10
  11.9 0.1 reshape.24.cols_ref
  12.1 0.7 fusion.copy_ref
  12.8 0.7 fusion.1.copy_ref
  13.6 14.2 %all-to-all-done.held_ref = bf16[128,24,128]{2,1,0:T(8,128)(2,1)S(1)} async-done(((bf16[128,24,128]{2,1,0:T(8,128)(2,1)}), bf16[128,24,128]{2,1,0:T(8,128)(2,1)S(1)}, u32[]{:S(2)}, u32[]{:S(2)}) %all-to-all-start) | async-done | bytes 786464 | tf_op jit(solution)/shard_map/all_to_all | solution.py:289
  27.7 1.8 %shard_map.64 = bf16[128,6,24,128]{3,2,1,0:T(8,128)(2,1)S(1)} custom-call(s32[768]{0:T(1024)S(1)} %dynamic-slice_reduce_fusion.route_ref, bf16[128,24,128]{2,1,0:T(8,128)(2,1)S(1)} %all-to-all-done.held_ref), custom_call_target="tpu_custom_call" | custom-call | bytes 9437184 | tf_op jit(solution)/shard_map/pallas_call | solution.py:145
  29.5 2.2 %copy-done = bf16[128,6,24,128]{3,2,1,0:T(8,128)(2,1)} copy-done((bf16[128,6,24,128]{3,2,1,0:T(8,128)(2,1)}, bf16[128,6,24,128]{3,2,1,0:T(8,128)(2,1)S(1)}, u32[]{:S(2)}) %copy-start) | copy-done | bytes 4718616
  31.7 5.5 %all-to-all-start.1 = ((bf16[128,6,24,128]{3,2,1,0:T(8,128)(2,1)}), bf16[128,6,24,128]{3,2,1,0:T(8,128)(2,1)}, u32[]{:S(2)}, u32[]{:S(2)}) async-start(bf16[128,6,24,128]{3,2,1,0:T(8,128)(2,1)} %copy-done), calls=%async_computation.1 | async-start | bytes 9437184 | tf_op jit(solution)/shard_map/all_to_all | solution.py:301
  37.2 62.3 %all-to-all-done.1 = bf16[128,6,24,128]{3,2,1,0:T(8,128)(2,1)} async-done(((bf16[128,6,24,128]{3,2,1,0:T(8,128)(2,1)}), bf16[128,6,24,128]{3,2,1,0:T(8,128)(2,1)}, u32[]{:S(2)}, u32[]{:S(2)}) %all-to-all-start.1) | async-done | bytes 4718624 | tf_op jit(solution)/shard_map/all_to_all | solution.py:301
  99.5 3.6 %constant_dynamic-slice_fusion.2 = (bf16[1,64,4,24,128]{4,3,2,1,0:T(8,128)(2,1)S(1)}, bf16[1,64,4,24,128]{4,3,2,1,0:T(8,128)(2,1)}) fusion(bf16[2,64,6,24,128]{4,3,2,1,0:T(8,128)(2,1)} %bitcast.5, s32[]{:T(128)S(6)} %select_n.40, s32[]{:T(128)S(6)} %select_n.39), kind=kLoop, calls=%fused_computation.5 | loop fusion | bytes 6291464 | tf_op jit(solution)/shard_map/slice | solution.py:305
  103.1 0.3 copy.22
  103.3 0.1 collective-permute-start.3
  103.4 1.8 %fusion.3 = (bf16[3,1,64,24,128]{4,3,2,0,1:T(8,128)(2,1)}, bf16[3,1,64,24,128]{4,3,2,0,1:T(8,128)(2,1)}) fusion(bf16[4,1,64,24,128]{4,3,2,0,1:T(8,128)(2,1)S(1)} %bitcast.23), kind=kLoop, calls=%fused_computation.14 | loop fusion | bytes 4718592 | tf_op jit(solution)/shard_map/slice | solution.py:310
  105.2 0.3 collective-permute-start
  105.6 0.3 collective-permute-start.1
  105.8 1.7 %slice.36 = bf16[2,64,2,24,128]{4,3,2,1,0:T(8,128)(2,1)S(1)} slice(bf16[2,64,6,24,128]{4,3,2,1,0:T(8,128)(2,1)} %bitcast.5), slice={[0:2], [0:64], [4:6], [0:24], [0:128]} | slice | bytes 3145728 | tf_op jit(solution)/shard_map/slice | solution.py:305
  107.5 0.3 copy.15
  107.8 1.1 copy-done.1
  108.9 0.3 copy.17
  109.3 0.1 pad_maximum_fusion
  109.4 0.5 collective-permute-start.2
  109.9 9.8 %shard_map.65.refs_6_ = f32[2,1,12,8,128,128]{5,4,3,2,1,0:T(8,128)S(1)} custom-call(s32[3072]{0:T(1024)S(1)} %reshape.24.cols_ref, s32[192]{0:T(256)S(1)} %reshape.25.kept_ref, s32[2]{0:T(128)S(1)} %pad_add_fusion.place_ref, s32[24]{0:T(128)S(1)} %fusion.copy_ref, bf16[4,12,128,128]{3,2,1,0:T(8,128)(2,1)S(1)} %bitcast.26, ...), custom_call_target="tpu_custom_call" | custom-call | flops 805306368 | bytes 26214400 | tf_op jit(solution)/shard_map/pallas_call | solution.py:246
  119.7 7.9 %collective-permute-done.2.refs_2_ = bf16[2,12,128,128]{3,2,1,0:T(8,128)(2,1)S(1)} collective-permute-done((bf16[2,12,128,128]{3,2,1,0:T(8,128)(2,1)S(1)}, bf16[2,12,128,128]{3,2,1,0:T(8,128)(2,1)S(1)}, u32[]{:S(2)}, u32[]{:S(2)}) %collective-permute-start.2) | collective-permute-done | bytes 786464 | tf_op jit(solution)/shard_map/ppermute | solution.py:276
  127.6 5.1 %collective-permute-done.refs_3_ = bf16[3,12,128,128]{3,2,1,0:T(8,128)(2,1)S(1)} collective-permute-done((bf16[3,12,128,128]{3,2,1,0:T(8,128)(2,1)}, bf16[3,12,128,128]{3,2,1,0:T(8,128)(2,1)S(1)}, u32[]{:S(2)}, u32[]{:S(2)}) %collective-permute-start) | collective-permute-done | bytes 1179680 | tf_op jit(solution)/shard_map/ppermute | solution.py:276
  132.7 0.9 collective-permute-done.1.refs_4_
  133.6 1.0 slice.35
  134.7 4.4 %collective-permute-start.4 = (bf16[2,12,128,128]{3,2,1,0:T(8,128)(2,1)S(1)}, bf16[2,12,128,128]{3,2,1,0:T(8,128)(2,1)S(1)}, u32[]{:S(2)}, u32[]{:S(2)}) collective-permute-start(bf16[2,12,128,128]{3,2,1,0:T(8,128)(2,1)S(1)} %pad_maximum_fusion.1), channel_id=1, source_target_pairs={{0,1},{1,0},{2,3},{3,2},{4,5},{5,4},{6,7},{7,6},{8,9},{9,8},{10,11... | collective-permute-start | bytes 2359304 | tf_op jit(solution)/shard_map/ppermute | solution.py:276
  139.1 1.9 %collective-permute-done.4.refs_5_ = bf16[2,12,128,128]{3,2,1,0:T(8,128)(2,1)S(1)} collective-permute-done((bf16[2,12,128,128]{3,2,1,0:T(8,128)(2,1)S(1)}, bf16[2,12,128,128]{3,2,1,0:T(8,128)(2,1)S(1)}, u32[]{:S(2)}, u32[]{:S(2)}) %collective-permute-start.4) | collective-permute-done | bytes 786464 | tf_op jit(solution)/shard_map/ppermute | solution.py:276
  141.0 12.2 %shard_map.66 = bf16[2,1,12,8,128,128]{5,4,3,2,1,0:T(8,128)(2,1)} custom-call(s32[3072]{0:T(1024)S(1)} %reshape.24.cols_ref, s32[192]{0:T(256)S(1)} %reshape.25.kept_ref, s32[2]{0:T(128)S(1)} %pad_add_fusion.place_ref, s32[28]{0:T(128)S(1)} %fusion.1.copy_ref, bf16[4,12,128,128]{3,2,1,0:T(8,128)(2,1)S(1)} %bitcast.27, ...), custom_call_target="tpu_custom_call" | custom-call | flops 805306368 | bytes 26214400 | tf_op jit(solution)/shard_map/pallas_call | solution.py:246
  (14 shorter events, 0.3 us)
Async XLA Ops:
  0.0 12.1 %copy-start.4 = (s32[2,768]{1,0:T(2,128)S(1)}, s32[2,768]{1,0:T(2,128)}, u32[]{:S(2)}) copy-start(s32[2,768]{1,0:T(2,128)} %constant.57.clone) | copy-start | bytes 18436
  0.0 11.6 %copy-start.3 = (s32[2,1,12,8]{2,3,1,0:T(8,128)S(1)}, s32[2,1,12,8]{2,3,1,0:T(8,128)}, u32[]{:S(2)}) copy-start(s32[2,1,12,8]{2,3,1,0:T(8,128)} %param.8) | copy-start | bytes 2308
  0.0 11.7 %copy-start.2 = (s32[16,16,12]{1,0,2:T(8,128)S(1)}, s32[16,16,12]{1,0,2:T(8,128)}, u32[]{:S(2)}) copy-start(s32[16,16,12]{1,0,2:T(8,128)} %param.7) | copy-start | bytes 36868
  0.0 27.7 %all-to-all-start = ((bf16[128,24,128]{2,1,0:T(8,128)(2,1)}), bf16[128,24,128]{2,1,0:T(8,128)(2,1)S(1)}, u32[]{:S(2)}, u32[]{:S(2)}) async-start(bf16[128,24,128]{2,1,0:T(8,128)(2,1)} %bitcast.31), calls=%async_computation | async-start | bytes 1572864 | tf_op jit(solution)/shard_map/all_to_all | solution.py:289
  29.5 2.2 %copy-start = (bf16[128,6,24,128]{3,2,1,0:T(8,128)(2,1)}, bf16[128,6,24,128]{3,2,1,0:T(8,128)(2,1)S(1)}, u32[]{:S(2)}) copy-start(bf16[128,6,24,128]{3,2,1,0:T(8,128)(2,1)S(1)} %shard_map.64) | copy-start | bytes 14155780
  31.7 67.8 %all-to-all-start.1 = ((bf16[128,6,24,128]{3,2,1,0:T(8,128)(2,1)}), bf16[128,6,24,128]{3,2,1,0:T(8,128)(2,1)}, u32[]{:S(2)}, u32[]{:S(2)}) async-start(bf16[128,6,24,128]{3,2,1,0:T(8,128)(2,1)} %copy-done), calls=%async_computation.1 | async-start | bytes 9437184 | tf_op jit(solution)/shard_map/all_to_all | solution.py:301
  103.3 6.5 %collective-permute-start.3 = (bf16[4,12,128,128]{3,2,1,0:T(8,128)(2,1)S(1)}, bf16[4,12,128,128]{3,2,1,0:T(8,128)(2,1)}, u32[]{:S(2)}, u32[]{:S(2)}) collective-permute-start(bf16[4,12,128,128]{3,2,1,0:T(8,128)(2,1)S(1)} %bitcast.22), channel_id=1, source_target_pairs={{0,1},{1,0},{2,3},{3,2},{4,5},{5,4},{6,7},{7,6},{8,9},{9,8},{10,11... | collective-permute-start | bytes 4718600 | tf_op jit(solution)/shard_map/ppermute | solution.py:276
  105.2 27.4 %collective-permute-start = (bf16[3,12,128,128]{3,2,1,0:T(8,128)(2,1)}, bf16[3,12,128,128]{3,2,1,0:T(8,128)(2,1)S(1)}, u32[]{:S(2)}, u32[]{:S(2)}) collective-permute-start(bf16[3,12,128,128]{3,2,1,0:T(8,128)(2,1)} %bitcast.11), channel_id=1, source_target_pairs={{0,2},{1,15},{2,4},{3,1},{4,6},{5,3},{6,8},{7,5},{8,10},{9,7},{10,... | collective-permute-start | bytes 3538952 | tf_op jit(solution)/shard_map/ppermute | solution.py:276
  105.6 28.0 %collective-permute-start.1 = (bf16[3,12,128,128]{3,2,1,0:T(8,128)(2,1)}, bf16[3,12,128,128]{3,2,1,0:T(8,128)(2,1)}, u32[]{:S(2)}, u32[]{:S(2)}) collective-permute-start(bf16[3,12,128,128]{3,2,1,0:T(8,128)(2,1)} %bitcast.12), channel_id=1, source_target_pairs={{0,15},{1,2},{2,1},{3,4},{4,3},{5,6},{6,5},{7,8},{8,7},{9,10},{10,... | collective-permute-start | bytes 3538952 | tf_op jit(solution)/shard_map/ppermute | solution.py:276
  107.5 1.4 copy-start.1
  109.4 18.2 %collective-permute-start.2 = (bf16[2,12,128,128]{3,2,1,0:T(8,128)(2,1)S(1)}, bf16[2,12,128,128]{3,2,1,0:T(8,128)(2,1)S(1)}, u32[]{:S(2)}, u32[]{:S(2)}) collective-permute-start(bf16[2,12,128,128]{3,2,1,0:T(8,128)(2,1)S(1)} %pad_maximum_fusion), channel_id=1, source_target_pairs={{0,16},{1,17},{2,18},{3,19},{4,20},{5,21},{6,22},{7,23},{8,24},{9,... | collective-permute-start | bytes 2359304 | tf_op jit(solution)/shard_map/ppermute | solution.py:276
  134.7 6.3 %collective-permute-start.4 = (bf16[2,12,128,128]{3,2,1,0:T(8,128)(2,1)S(1)}, bf16[2,12,128,128]{3,2,1,0:T(8,128)(2,1)S(1)}, u32[]{:S(2)}, u32[]{:S(2)}) collective-permute-start(bf16[2,12,128,128]{3,2,1,0:T(8,128)(2,1)S(1)} %pad_maximum_fusion.1), channel_id=1, source_target_pairs={{0,1},{1,0},{2,3},{3,2},{4,5},{5,4},{6,7},{7,6},{8,9},{9,8},{10,11... | collective-permute-start | bytes 2359304 | tf_op jit(solution)/shard_map/ppermute | solution.py:276

commit v2 on v1

--- a/solution.py
+++ b/solution.py
@@ -156,6 +156,44 @@
             flops=0, bytes_accessed=2 * DEVICES * PAIRS * PIECE * SIDE * 2, transcendentals=0
         ),
     )(route, held)
+
+
+def split_kernel(half_ref, received_ref, left_ref, forward_ref, backward_ref):
+    count = left_ref.shape[0]
+    for pair in range(count):
+        pieces = received_ref[0, :, pair]
+        left_ref[pair] = pieces
+        if pair + 1 < count:
+            forward_ref[pair] = pieces
+        if pair:
+            backward_ref[pair - 1] = pieces
+
+
+def split(received, half, count):
+    group = 16
+    sizes = (count, count - 1, count - 1)
+    results = pl.pallas_call(
+        split_kernel,
+        grid_spec=pltpu.PrefetchScalarGridSpec(
+            num_scalar_prefetch=1,
+            grid=(HOLDERS // group,),
+            in_specs=[
+                pl.BlockSpec(
+                    (1, group, count, PIECE, SIDE), lambda t, half: (half[0], t, 0, 0, 0)
+                )
+            ],
+            out_specs=[
+                pl.BlockSpec((size, group, PIECE, SIDE), lambda t, half: (0, t, 0, 0))
+                for size in sizes
+            ],
+        ),
+        out_shape=[
+            jax.ShapeDtypeStruct((size, HOLDERS, PIECE, SIDE), received.dtype) for size in sizes
+        ],
+        compiler_params=pltpu.CompilerParams(vmem_limit_bytes=16 << 20),
+        cost_estimate=pl.CostEstimate(flops=0, bytes_accessed=6 << 20, transcendentals=0),
+    )(half.reshape(1), received)
+    return [array.reshape(-1, TILE, SIDE, SIDE) for array in results]
 
 
 def matmul(left, right, right_dim):
@@ -210,7 +248,6 @@
         rels = (jnp.where(edge == 2, 4, edge), jnp.where(edge == 0, 1, 3 + edge))
     else:
         rels = CENTRE
-    terms = []
     for sub in range(lines):
         line = step * lines % TILE + sub
         for rel in rels:
@@ -221,11 +258,10 @@
             mirror = tiles[LEFT_MIRROR + 2 * rel + slot, mirror_col].T
             for left, middle in ((own, own_col), (mirror, mirror_col)):
                 flipped = right_inv[rel * TILE + middle]
-                straight = matmul(left, tiles[RIGHT_OWN + rel, middle], 0)
-                terms.append((sub, entry(ahead, col, middle), straight))
-                terms.append((sub, flipped, matmul(left, tiles[RIGHT_MIRROR + rel, flipped], 1)))
-    for sub, target, term in terms:
-        total[sub, target] += term
+                total[sub, entry(ahead, col, middle)] += matmul(
+                    left, tiles[RIGHT_OWN + rel, middle], 0
+                )
+                total[sub, flipped] += matmul(left, tiles[RIGHT_MIRROR + rel, flipped], 1)
     for sub in range(lines):
         for o in range(kept_count):
             value = total[sub, kept_ref[(step * lines + sub) * kept_count + o]]
@@ -305,9 +341,9 @@
         pieces = pieces[:, :, start : start + count].transpose(2, 0, 1, 3, 4)
         return pieces.reshape(-1, TILE, SIDE, SIDE)
 
-    left = gathered(one(received, 1 - core), 0, 4)
-    forward = moved(left[:3], lambda r, m, c: (r, m + 1 - 2 * c, c))
-    backward = moved(left[1:], lambda r, m, c: (r, m - 1 + 2 * c, 1 - c))
+    left, forward, backward = split(received, 1 - core, 4)
+    forward = moved(forward, lambda r, m, c: (r, m + 1 - 2 * c, c))
+    backward = moved(backward, lambda r, m, c: (r, m - 1 + 2 * c, 1 - c))
     sibling = moved(left, lambda r, m, c: (r, m, 1 - c))
     mirror = gathered(one(received, core), 0, 4)
     own = gathered(received, 4, 2)

time: 154 us -> 151 us (0.981)
  waiting for transfers between devices: 92.3 us -> 87.6 us
  local copies, waits for them, and re-layouts: 14.2 us -> 9.53 us
  starting transfers between devices: 22.5 us -> 27 us
  Pallas kernels: 23.7 us -> 25.9 us
    slice x3 -> x0, local copies, waits for them, and re-layouts: 7.08 us -> none  [the longest x2 5.27 us: gathered(): pieces = pieces[:, :, start:start + count].transpose(2, 0, 1, 3, 4)]
    ppermute x5, waiting for transfers between devices: 15.8 us -> 11.1 us  [moved(): return lax.ppermute(tiles, AXES, pairs)]
    ppermute x5, starting transfers between devices: 5.56 us -> 10 us  [moved(): return lax.ppermute(tiles, AXES, pairs)]
    transpose x0 -> x4, local copies, waits for them, and re-layouts: none -> 3.93 us  [gathered(): pieces = pieces[:, :, start:start + count].transpose(2, 0, 1, 3, 4)]
    pallas_call x0 -> x1, Pallas kernels: none -> 2.67 us  [split(): pl.pallas_call(split_kernel, grid_spec=pltpu.PrefetchScalarGridSpec(num_s...]
    unnamed x15 -> x14, local copies, waits for them, and re-layouts: 4.39 us -> 3.87 us
  transfers between devices with their start and end apart: 7 -> 7, of which waited for: 6 -> 5; matrix products, arithmetic and copies ran while one was open for 4% -> 4% of each run, Pallas kernels for 6% -> 6%
where the time goes in v2:
time: 151 us; the launch traced here: 150 us
  waiting for transfers between devices  87.6 us (58%)
  starting transfers between devices  27 us (18%)
  Pallas kernels  25.9 us (17%)
  local copies, waits for them, and re-layouts  9.53 us (6%)
    all_to_all x1, waiting for transfers between devices, on_device(): lax.all_to_all(outgoing, AXES, split_axis=0, concat_axis=0, tiled=True)  62.3 us
    pallas_call x2, Pallas kernels, products(): pl.pallas_call(functools.partial(product_kernel, len(arrays), from_arrays...  21.5 us
    all_to_all x1, waiting for transfers between devices, on_device(): held = lax.all_to_all(spread, AXES, split_axis=0, concat_axis=0, tiled=True)  14.2 us
    all_to_all x1, starting transfers between devices, on_device(): held = lax.all_to_all(spread, AXES, split_axis=0, concat_axis=0, tiled=True)  11.5 us
    ppermute x5, waiting for transfers between devices, moved(): return lax.ppermute(tiles, AXES, pairs)  11.1 us
    ppermute x5, starting transfers between devices, moved(): return lax.ppermute(tiles, AXES, pairs)  10 us
    all_to_all x1, starting transfers between devices, on_device(): lax.all_to_all(outgoing, AXES, split_axis=0, concat_axis=0, tiled=True)  5.47 us
    transpose x4, local copies, waits for them, and re-layouts, gathered(): pieces = pieces[:, :, start:start + count].transpose(2, 0, 1, 3, 4)  3.93 us
  transfers between devices with their start and end apart: 7, of which 5 were waited for; matrix products, arithmetic and copies ran while one was open for 4% of the time, Pallas kernels for 6%

profile of v2, /device:TPU:1, one launch (start us, length us, event | category | flops | bytes accessed | tf_op | source)
XLA Modules:
  0.0 150.5 jit_solution(5121437163227381007)
XLA Ops:
  0.0 11.5 %all-to-all-start = ((bf16[128,24,128]{2,1,0:T(8,128)(2,1)}), bf16[128,24,128]{2,1,0:T(8,128)(2,1)S(1)}, u32[]{:S(2)}, u32[]{:S(2)}) async-start(bf16[128,24,128]{2,1,0:T(8,128)(2,1)} %bitcast.30), calls=%async_computation | async-start | bytes 1572864 | tf_op jit(solution)/shard_map/all_to_all | solution.py:325
  11.6 0.1 copy.10
  11.7 0.1 reshape.32.kept_ref
  11.8 0.2 copy.9
  11.9 0.1 reshape.31.cols_ref
  12.1 0.7 fusion.copy_ref
  12.8 0.7 fusion.1.copy_ref
  13.5 0.1 pad_add_fusion.place_ref
  13.6 14.2 %all-to-all-done.held_ref = bf16[128,24,128]{2,1,0:T(8,128)(2,1)S(1)} async-done(((bf16[128,24,128]{2,1,0:T(8,128)(2,1)}), bf16[128,24,128]{2,1,0:T(8,128)(2,1)S(1)}, u32[]{:S(2)}, u32[]{:S(2)}) %all-to-all-start) | async-done | bytes 786464 | tf_op jit(solution)/shard_map/all_to_all | solution.py:325
  27.7 1.8 %shard_map.64 = bf16[128,6,24,128]{3,2,1,0:T(8,128)(2,1)S(1)} custom-call(s32[768]{0:T(1024)S(1)} %dynamic-slice_reduce_fusion.route_ref, bf16[128,24,128]{2,1,0:T(8,128)(2,1)S(1)} %all-to-all-done.held_ref), custom_call_target="tpu_custom_call" | custom-call | bytes 9437184 | tf_op jit(solution)/shard_map/pallas_call | solution.py:145
  29.5 0.0 copy-start
  29.5 2.2 %copy-done = bf16[128,6,24,128]{3,2,1,0:T(8,128)(2,1)} copy-done((bf16[128,6,24,128]{3,2,1,0:T(8,128)(2,1)}, bf16[128,6,24,128]{3,2,1,0:T(8,128)(2,1)S(1)}, u32[]{:S(2)}) %copy-start) | copy-done | bytes 4718616
  31.7 5.5 %all-to-all-start.1 = ((bf16[128,6,24,128]{3,2,1,0:T(8,128)(2,1)}), bf16[128,6,24,128]{3,2,1,0:T(8,128)(2,1)}, u32[]{:S(2)}, u32[]{:S(2)}) async-start(bf16[128,6,24,128]{3,2,1,0:T(8,128)(2,1)} %copy-done), calls=%async_computation.1 | async-start | bytes 9437184 | tf_op jit(solution)/shard_map/all_to_all | solution.py:337
  37.2 62.3 %all-to-all-done.1 = bf16[128,6,24,128]{3,2,1,0:T(8,128)(2,1)} async-done(((bf16[128,6,24,128]{3,2,1,0:T(8,128)(2,1)}), bf16[128,6,24,128]{3,2,1,0:T(8,128)(2,1)}, u32[]{:S(2)}, u32[]{:S(2)}) %all-to-all-start.1) | async-done | bytes 4718624 | tf_op jit(solution)/shard_map/all_to_all | solution.py:337
  99.5 2.7 %shard_map.65 = (bf16[4,64,24,128]{3,2,1,0:T(8,128)(2,1)S(1)}, bf16[3,64,24,128]{3,2,1,0:T(8,128)(2,1)S(1)}, bf16[3,64,24,128]{3,2,1,0:T(8,128)(2,1)S(1)}) custom-call(s32[1]{0:T(128)} %bitcast.10.half_ref, bf16[2,64,6,24,128]{4,3,2,1,0:T(8,128)(2,1)} %bitcast.5.received_ref), custom_call_target="tpu_custom_call" | custom-call | bytes 6291456 | tf_op jit(solution)/shard_map/pallas_call | solution.py:175
  102.2 1.0 copy-done.1
  103.2 0.4 copy-done.2
  103.6 5.5 %collective-permute-start = (bf16[3,12,128,128]{3,2,1,0:T(8,128)(2,1)}, bf16[3,12,128,128]{3,2,1,0:T(8,128)(2,1)S(1)}, u32[]{:S(2)}, u32[]{:S(2)}) collective-permute-start(bf16[3,12,128,128]{3,2,1,0:T(8,128)(2,1)} %bitcast.28), channel_id=1, source_target_pairs={{0,2},{1,15},{2,4},{3,1},{4,6},{5,3},{6,8},{7,5},{8,10},{9,7},{10,... | collective-permute-start | bytes 3538952 | tf_op jit(solution)/shard_map/ppermute | solution.py:312
  109.1 1.7 %slice_bitcast_fusion = bf16[2,2,64,24,128]{4,3,0,2,1:T(8,128)(2,1)S(1)} fusion(bf16[2,64,6,24,128]{4,3,2,1,0:T(8,128)(2,1)} %bitcast.5.received_ref), kind=kLoop, calls=%fused_computation.1 | loop fusion | bytes 3145728 | tf_op jit(solution)/shard_map/transpose | solution.py:341
  110.8 1.7 %dynamic-slice_bitcast_fusion = bf16[4,1,64,24,128]{4,3,0,2,1:T(8,128)(2,1)S(1)} fusion(bf16[2,64,6,24,128]{4,3,2,1,0:T(8,128)(2,1)} %bitcast.5.received_ref, s32[]{:T(128)S(6)} %select_n.36), kind=kLoop, calls=%fused_computation | loop fusion | bytes 3145732 | tf_op jit(solution)/shard_map/transpose | solution.py:341
  112.5 0.3 copy.12
  112.8 0.3 copy.11
  113.0 0.1 constant_dynamic-slice_fusion
  113.1 0.1 pad_maximum_fusion
  113.2 0.1 collective-permute-start.2
  113.3 9.4 %shard_map.66.refs_6_ = f32[2,1,12,8,128,128]{5,4,3,2,1,0:T(8,128)S(1)} custom-call(s32[3072]{0:T(1024)S(1)} %reshape.31.cols_ref, s32[192]{0:T(256)S(1)} %reshape.32.kept_ref, s32[2]{0:T(128)S(1)} %pad_add_fusion.place_ref, s32[24]{0:T(128)S(1)} %fusion.copy_ref, bf16[4,12,128,128]{3,2,1,0:T(8,128)(2,1)S(1)} %bitcast.24, ...), custom_call_target="tpu_custom_call" | custom-call | flops 805306368 | bytes 26214400 | tf_op jit(solution)/shard_map/pallas_call | solution.py:282
  122.7 7.3 %collective-permute-done.2.refs_2_ = bf16[2,12,128,128]{3,2,1,0:T(8,128)(2,1)S(1)} collective-permute-done((bf16[2,12,128,128]{3,2,1,0:T(8,128)(2,1)S(1)}, bf16[2,12,128,128]{3,2,1,0:T(8,128)(2,1)S(1)}, u32[]{:S(2)}, u32[]{:S(2)}) %collective-permute-start.2) | collective-permute-done | bytes 786464 | tf_op jit(solution)/shard_map/ppermute | solution.py:312
  130.0 1.9 %collective-permute-done.1.refs_4_ = bf16[3,12,128,128]{3,2,1,0:T(8,128)(2,1)S(1)} collective-permute-done((bf16[3,12,128,128]{3,2,1,0:T(8,128)(2,1)}, bf16[3,12,128,128]{3,2,1,0:T(8,128)(2,1)S(1)}, u32[]{:S(2)}, u32[]{:S(2)}) %collective-permute-start.1) | collective-permute-done | bytes 1179680 | tf_op jit(solution)/shard_map/ppermute | solution.py:312
  131.9 0.1 pad_maximum_fusion.1
  132.0 4.4 %collective-permute-start.4 = (bf16[2,12,128,128]{3,2,1,0:T(8,128)(2,1)S(1)}, bf16[2,12,128,128]{3,2,1,0:T(8,128)(2,1)S(1)}, u32[]{:S(2)}, u32[]{:S(2)}) collective-permute-start(bf16[2,12,128,128]{3,2,1,0:T(8,128)(2,1)S(1)} %pad_maximum_fusion.1), channel_id=1, source_target_pairs={{0,1},{1,0},{2,3},{3,2},{4,5},{5,4},{6,7},{7,6},{8,9},{9,8},{10,11... | collective-permute-start | bytes 2359304 | tf_op jit(solution)/shard_map/ppermute | solution.py:312
  136.4 1.9 %collective-permute-done.4.refs_5_ = bf16[2,12,128,128]{3,2,1,0:T(8,128)(2,1)S(1)} collective-permute-done((bf16[2,12,128,128]{3,2,1,0:T(8,128)(2,1)S(1)}, bf16[2,12,128,128]{3,2,1,0:T(8,128)(2,1)S(1)}, u32[]{:S(2)}, u32[]{:S(2)}) %collective-permute-start.4) | collective-permute-done | bytes 786464 | tf_op jit(solution)/shard_map/ppermute | solution.py:312
  138.4 12.1 %shard_map.67 = bf16[2,1,12,8,128,128]{5,4,3,2,1,0:T(8,128)(2,1)} custom-call(s32[3072]{0:T(1024)S(1)} %reshape.31.cols_ref, s32[192]{0:T(256)S(1)} %reshape.32.kept_ref, s32[2]{0:T(128)S(1)} %pad_add_fusion.place_ref, s32[28]{0:T(128)S(1)} %fusion.1.copy_ref, bf16[4,12,128,128]{3,2,1,0:T(8,128)(2,1)S(1)} %bitcast.25, ...), custom_call_target="tpu_custom_call" | custom-call | flops 805306368 | bytes 26214400 | tf_op jit(solution)/shard_map/pallas_call | solution.py:282
  (15 shorter events, 0.1 us)
Async XLA Ops:
  0.0 12.1 %copy-start.5 = (s32[2,768]{1,0:T(2,128)S(1)}, s32[2,768]{1,0:T(2,128)}, u32[]{:S(2)}) copy-start(s32[2,768]{1,0:T(2,128)} %constant.55.clone) | copy-start | bytes 18436
  0.0 11.6 %copy-start.4 = (s32[2,1,12,8]{2,3,1,0:T(8,128)S(1)}, s32[2,1,12,8]{2,3,1,0:T(8,128)}, u32[]{:S(2)}) copy-start(s32[2,1,12,8]{2,3,1,0:T(8,128)} %param.8) | copy-start | bytes 2308
  0.0 11.7 %copy-start.3 = (s32[16,16,12]{1,0,2:T(8,128)S(1)}, s32[16,16,12]{1,0,2:T(8,128)}, u32[]{:S(2)}) copy-start(s32[16,16,12]{1,0,2:T(8,128)} %param.7) | copy-start | bytes 36868
  0.0 27.7 %all-to-all-start = ((bf16[128,24,128]{2,1,0:T(8,128)(2,1)}), bf16[128,24,128]{2,1,0:T(8,128)(2,1)S(1)}, u32[]{:S(2)}, u32[]{:S(2)}) async-start(bf16[128,24,128]{2,1,0:T(8,128)(2,1)} %bitcast.30), calls=%async_computation | async-start | bytes 1572864 | tf_op jit(solution)/shard_map/all_to_all | solution.py:325
  29.5 2.2 %copy-start = (bf16[128,6,24,128]{3,2,1,0:T(8,128)(2,1)}, bf16[128,6,24,128]{3,2,1,0:T(8,128)(2,1)S(1)}, u32[]{:S(2)}) copy-start(bf16[128,6,24,128]{3,2,1,0:T(8,128)(2,1)S(1)} %shard_map.64) | copy-start | bytes 14155780
  31.7 67.8 %all-to-all-start.1 = ((bf16[128,6,24,128]{3,2,1,0:T(8,128)(2,1)}), bf16[128,6,24,128]{3,2,1,0:T(8,128)(2,1)}, u32[]{:S(2)}, u32[]{:S(2)}) async-start(bf16[128,6,24,128]{3,2,1,0:T(8,128)(2,1)} %copy-done), calls=%async_computation.1 | async-start | bytes 9437184 | tf_op jit(solution)/shard_map/all_to_all | solution.py:337
  102.2 1.0 copy-start.1
  102.2 1.4 copy-start.2
  103.6 9.7 %collective-permute-start.3 = (bf16[4,12,128,128]{3,2,1,0:T(8,128)(2,1)S(1)}, bf16[4,12,128,128]{3,2,1,0:T(8,128)(2,1)S(1)}, u32[]{:S(2)}, u32[]{:S(2)}) collective-permute-start(bf16[4,12,128,128]{3,2,1,0:T(8,128)(2,1)S(1)} %bitcast.26), channel_id=1, source_target_pairs={{0,1},{1,0},{2,3},{3,2},{4,5},{5,4},{6,7},{7,6},{8,9},{9,8},{10,11... | collective-permute-start | bytes 4718600 | tf_op jit(solution)/shard_map/ppermute | solution.py:312
  103.6 28.2 %collective-permute-start.1 = (bf16[3,12,128,128]{3,2,1,0:T(8,128)(2,1)}, bf16[3,12,128,128]{3,2,1,0:T(8,128)(2,1)S(1)}, u32[]{:S(2)}, u32[]{:S(2)}) collective-permute-start(bf16[3,12,128,128]{3,2,1,0:T(8,128)(2,1)} %bitcast.29), channel_id=1, source_target_pairs={{0,15},{1,2},{2,1},{3,4},{4,3},{5,6},{6,5},{7,8},{8,7},{9,10},{10,... | collective-permute-start | bytes 3538952 | tf_op jit(solution)/shard_map/ppermute | solution.py:312
  103.6 28.2 %collective-permute-start = (bf16[3,12,128,128]{3,2,1,0:T(8,128)(2,1)}, bf16[3,12,128,128]{3,2,1,0:T(8,128)(2,1)S(1)}, u32[]{:S(2)}, u32[]{:S(2)}) collective-permute-start(bf16[3,12,128,128]{3,2,1,0:T(8,128)(2,1)} %bitcast.28), channel_id=1, source_target_pairs={{0,2},{1,15},{2,4},{3,1},{4,6},{5,3},{6,8},{7,5},{8,10},{9,7},{10,... | collective-permute-start | bytes 3538952 | tf_op jit(solution)/shard_map/ppermute | solution.py:312
  113.2 16.8 %collective-permute-start.2 = (bf16[2,12,128,128]{3,2,1,0:T(8,128)(2,1)S(1)}, bf16[2,12,128,128]{3,2,1,0:T(8,128)(2,1)S(1)}, u32[]{:S(2)}, u32[]{:S(2)}) collective-permute-start(bf16[2,12,128,128]{3,2,1,0:T(8,128)(2,1)S(1)} %pad_maximum_fusion), channel_id=1, source_target_pairs={{0,16},{1,17},{2,18},{3,19},{4,20},{5,21},{6,22},{7,23},{8,24},{9,... | collective-permute-start | bytes 2359304 | tf_op jit(solution)/shard_map/ppermute | solution.py:312
  132.0 6.4 %collective-permute-start.4 = (bf16[2,12,128,128]{3,2,1,0:T(8,128)(2,1)S(1)}, bf16[2,12,128,128]{3,2,1,0:T(8,128)(2,1)S(1)}, u32[]{:S(2)}, u32[]{:S(2)}) collective-permute-start(bf16[2,12,128,128]{3,2,1,0:T(8,128)(2,1)S(1)} %pad_maximum_fusion.1), channel_id=1, source_target_pairs={{0,1},{1,0},{2,3},{3,2},{4,5},{5,4},{6,7},{7,6},{8,9},{9,8},{10,11... | collective-permute-start | bytes 2359304 | tf_op jit(solution)/shard_map/ppermute | solution.py:312

commit v3 on v2

--- a/solution.py
+++ b/solution.py
@@ -73,10 +73,11 @@
     missing = core if high else core + 4
     copies += [(2, 0, slot_of(RIGHT_OWN, missing)), (2, 1, slot_of(RIGHT_MIRROR, missing))]
     first, second = from_neighbours(core)
-    copies += [(3, i, slot_of(*tile)) for i, tile in enumerate(first)]
-    copies += [(4, i, slot_of(*tile)) for i, tile in enumerate(second)]
+    copies += [(3, 0, slot_of(*first[0])), (4, 0, slot_of(*second[2]))]
+    copies += [(5, i, slot_of(*tile)) for i, tile in enumerate(first[1:])]
+    copies += [(6, i, slot_of(*tile)) for i, tile in enumerate(second[:2])]
     first, second = from_neighbours(1 - core)
-    copies += [(5, 0, slot_of(*first[0])), (5, 1, slot_of(*second[2]))]
+    copies += [(7, 0, slot_of(*first[0])), (7, 1, slot_of(*second[2]))]
     return copies
 
 
@@ -158,29 +159,25 @@
     )(route, held)
 
 
-def split_kernel(half_ref, received_ref, left_ref, forward_ref, backward_ref):
-    count = left_ref.shape[0]
-    for pair in range(count):
-        pieces = received_ref[0, :, pair]
-        left_ref[pair] = pieces
-        if pair + 1 < count:
-            forward_ref[pair] = pieces
-        if pair:
-            backward_ref[pair - 1] = pieces
-
-
-def split(received, half, count):
+def split_kernel(half_ref, received_ref, left_ref, head_ref, middle_ref, tail_ref):
+    for pair in range(4):
+        left_ref[pair] = received_ref[0, :, pair]
+    head_ref[0] = received_ref[0, :, 0]
+    middle_ref[0] = received_ref[0, :, 1]
+    middle_ref[1] = received_ref[0, :, 2]
+    tail_ref[0] = received_ref[0, :, 3]
+
+
+def split(received, half):
     group = 16
-    sizes = (count, count - 1, count - 1)
+    sizes = (4, 1, 2, 1)
     results = pl.pallas_call(
         split_kernel,
         grid_spec=pltpu.PrefetchScalarGridSpec(
             num_scalar_prefetch=1,
             grid=(HOLDERS // group,),
             in_specs=[
-                pl.BlockSpec(
-                    (1, group, count, PIECE, SIDE), lambda t, half: (half[0], t, 0, 0, 0)
-                )
+                pl.BlockSpec((1, group, 4, PIECE, SIDE), lambda t, half: (half[0], t, 0, 0, 0))
             ],
             out_specs=[
                 pl.BlockSpec((size, group, PIECE, SIDE), lambda t, half: (0, t, 0, 0))
@@ -191,7 +188,7 @@
             jax.ShapeDtypeStruct((size, HOLDERS, PIECE, SIDE), received.dtype) for size in sizes
         ],
         compiler_params=pltpu.CompilerParams(vmem_limit_bytes=16 << 20),
-        cost_estimate=pl.CostEstimate(flops=0, bytes_accessed=6 << 20, transcendentals=0),
+        cost_estimate=pl.CostEstimate(flops=0, bytes_accessed=5 << 20, transcendentals=0),
     )(half.reshape(1), received)
     return [array.reshape(-1, TILE, SIDE, SIDE) for array in results]
 
@@ -341,9 +338,16 @@
         pieces = pieces[:, :, start : start + count].transpose(2, 0, 1, 3, 4)
         return pieces.reshape(-1, TILE, SIDE, SIDE)
 
-    left, forward, backward = split(received, 1 - core, 4)
-    forward = moved(forward, lambda r, m, c: (r, m + 1 - 2 * c, c))
-    backward = moved(backward, lambda r, m, c: (r, m - 1 + 2 * c, 1 - c))
+    left, head, middle, tail = split(received, 1 - core)
+
+    def forward(tiles):
+        return moved(tiles, lambda r, m, c: (r, m + 1 - 2 * c, c))
+
+    def backward(tiles):
+        return moved(tiles, lambda r, m, c: (r, m - 1 + 2 * c, 1 - c))
+
+    head, tail = forward(head), backward(tail)
+    ahead, behind = forward(middle), backward(middle)
     sibling = moved(left, lambda r, m, c: (r, m, 1 - c))
     mirror = gathered(one(received, core), 0, 4)
     own = gathered(received, 4, 2)
@@ -359,18 +363,14 @@
         copy_arrays(centre_copies),
         kept_count,
     )
-    forward, backward, across, partial = lax.optimization_barrier(
-        (forward, backward, across, partial)
-    )
-    shared = moved(
-        jnp.concatenate([forward[:1], backward[2:]], 0), lambda r, m, c: (r, m, 1 - c)
-    )
+    head, tail, partial = lax.optimization_barrier((head, tail, partial))
+    shared = moved(jnp.concatenate([head, tail], 0), lambda r, m, c: (r, m, 1 - c))
     return products(
         cols,
         kept,
         place,
         outer,
-        (own, mirror, across, forward, backward, shared),
+        (own, mirror, across, head, tail, ahead, behind, shared),
         copy_arrays(outer_copies),
         kept_count,
         partial,

time: 151 us -> 150 us (level)
  waiting for transfers between devices: 87.6 us -> 85.9 us
  starting transfers between devices: 27 us -> 28.6 us
    ppermute x5 -> x7, waiting for transfers between devices: 11.1 us -> 9.42 us  [moved(): return lax.ppermute(tiles, AXES, pairs)]
    ppermute x5 -> x7, starting transfers between devices: 10 us -> 11.6 us  [moved(): return lax.ppermute(tiles, AXES, pairs)]
    unnamed x14 -> x16, local copies, waits for them, and re-layouts: 3.87 us -> 3.59 us
  transfers between devices with their start and end apart: 7 -> 9, of which waited for: 5 -> 4; matrix products, arithmetic and copies ran while one was open for 4% -> 4% of each run, Pallas kernels for 6% -> 6%
where the time goes in v3:
time: 150 us
  waiting for transfers between devices  85.9 us (57%)
  starting transfers between devices  28.6 us (19%)
  Pallas kernels  25.8 us (17%)
  local copies, waits for them, and re-layouts  9.19 us (6%)
    all_to_all x1, waiting for transfers between devices, on_device(): lax.all_to_all(outgoing, AXES, split_axis=0, concat_axis=0, tiled=True)  62.3 us
    pallas_call x2, Pallas kernels, products(): pl.pallas_call(functools.partial(product_kernel, len(arrays), from_arrays...  21.5 us
    all_to_all x1, waiting for transfers between devices, on_device(): held = lax.all_to_all(spread, AXES, split_axis=0, concat_axis=0, tiled=True)  14.2 us
    ppermute x7, starting transfers between devices, moved(): return lax.ppermute(tiles, AXES, pairs)  11.6 us
    all_to_all x1, starting transfers between devices, on_device(): held = lax.all_to_all(spread, AXES, split_axis=0, concat_axis=0, tiled=True)  11.5 us
    ppermute x7, waiting for transfers between devices, moved(): return lax.ppermute(tiles, AXES, pairs)  9.42 us
    all_to_all x1, starting transfers between devices, on_device(): lax.all_to_all(outgoing, AXES, split_axis=0, concat_axis=0, tiled=True)  5.47 us
    transpose x4, local copies, waits for them, and re-layouts, gathered(): pieces = pieces[:, :, start:start + count].transpose(2, 0, 1, 3, 4)  3.93 us
  transfers between devices with their start and end apart: 9, of which 4 were waited for; matrix products, arithmetic and copies ran while one was open for 4% of the time, Pallas kernels for 6%

profile of v3, /device:TPU:1, one launch (start us, length us, event | category | flops | bytes accessed | tf_op | source)
XLA Modules:
  0.0 150.0 jit_solution(13910667145993929123)
XLA Ops:
  0.0 11.5 %all-to-all-start = ((bf16[128,24,128]{2,1,0:T(8,128)(2,1)}), bf16[128,24,128]{2,1,0:T(8,128)(2,1)S(1)}, u32[]{:S(2)}, u32[]{:S(2)}) async-start(bf16[128,24,128]{2,1,0:T(8,128)(2,1)} %bitcast.33), calls=%async_computation | async-start | bytes 1572864 | tf_op jit(solution)/shard_map/all_to_all | solution.py:322
  11.6 0.1 copy.10
  11.7 0.1 reshape.35.kept_ref
  11.8 0.2 copy.9
  11.9 0.1 reshape.34.cols_ref
  12.1 0.7 fusion.copy_ref
  12.8 0.7 fusion.1.copy_ref
  13.5 0.1 pad_add_fusion.place_ref
  13.6 14.2 %all-to-all-done.held_ref = bf16[128,24,128]{2,1,0:T(8,128)(2,1)S(1)} async-done(((bf16[128,24,128]{2,1,0:T(8,128)(2,1)}), bf16[128,24,128]{2,1,0:T(8,128)(2,1)S(1)}, u32[]{:S(2)}, u32[]{:S(2)}) %all-to-all-start) | async-done | bytes 786464 | tf_op jit(solution)/shard_map/all_to_all | solution.py:322
  27.7 1.8 %shard_map.64 = bf16[128,6,24,128]{3,2,1,0:T(8,128)(2,1)S(1)} custom-call(s32[768]{0:T(1024)S(1)} %dynamic-slice_reduce_fusion.route_ref, bf16[128,24,128]{2,1,0:T(8,128)(2,1)S(1)} %all-to-all-done.held_ref), custom_call_target="tpu_custom_call" | custom-call | bytes 9437184 | tf_op jit(solution)/shard_map/pallas_call | solution.py:146
  29.5 2.2 %copy-done = bf16[128,6,24,128]{3,2,1,0:T(8,128)(2,1)} copy-done((bf16[128,6,24,128]{3,2,1,0:T(8,128)(2,1)}, bf16[128,6,24,128]{3,2,1,0:T(8,128)(2,1)S(1)}, u32[]{:S(2)}) %copy-start) | copy-done | bytes 4718616
  31.7 5.5 %all-to-all-start.1 = ((bf16[128,6,24,128]{3,2,1,0:T(8,128)(2,1)}), bf16[128,6,24,128]{3,2,1,0:T(8,128)(2,1)}, u32[]{:S(2)}, u32[]{:S(2)}) async-start(bf16[128,6,24,128]{3,2,1,0:T(8,128)(2,1)} %copy-done), calls=%async_computation.1 | async-start | bytes 9437184 | tf_op jit(solution)/shard_map/all_to_all | solution.py:334
  37.2 62.3 %all-to-all-done.1 = bf16[128,6,24,128]{3,2,1,0:T(8,128)(2,1)} async-done(((bf16[128,6,24,128]{3,2,1,0:T(8,128)(2,1)}), bf16[128,6,24,128]{3,2,1,0:T(8,128)(2,1)}, u32[]{:S(2)}, u32[]{:S(2)}) %all-to-all-start.1) | async-done | bytes 4718624 | tf_op jit(solution)/shard_map/all_to_all | solution.py:334
  99.5 2.5 %shard_map.65 = (bf16[4,64,24,128]{3,2,1,0:T(8,128)(2,1)S(1)}, bf16[1,64,24,128]{3,2,1,0:T(8,128)(2,1)S(1)}, bf16[2,64,24,128]{3,2,1,0:T(8,128)(2,1)S(1)}, bf16[1,64,24,128]{3,2,1,0:T(8,128)(2,1)S(1)}) custom-call(s32[1]{0:T(128)} %bitcast.10.half_ref, bf16[2,64,6,24,128]{4,3,2,1,0:T(8,128)(2,1)} %bitcast.5.received_ref), custom_call_target="tpu_custom_call" | custom-call | bytes 5242880 | tf_op jit(solution)/shard_map/pallas_call | solution.py:174
  102.0 0.8 copy-done.1
  102.9 0.1 copy-done.2
  103.0 0.2 copy-done.3
  103.2 5.5 %collective-permute-start.4 = (bf16[2,12,128,128]{3,2,1,0:T(8,128)(2,1)}, bf16[2,12,128,128]{3,2,1,0:T(8,128)(2,1)S(1)}, u32[]{:S(2)}, u32[]{:S(2)}) collective-permute-start(bf16[2,12,128,128]{3,2,1,0:T(8,128)(2,1)} %bitcast.30), channel_id=1, source_target_pairs={{0,2},{1,15},{2,4},{3,1},{4,6},{5,3},{6,8},{7,5},{8,10},{9,7},{10,... | collective-permute-start | bytes 2359304 | tf_op jit(solution)/shard_map/ppermute | solution.py:309
  108.7 1.6 %collective-permute-start.1 = (bf16[1,12,128,128]{3,2,1,0:T(8,128)(2,1)}, bf16[1,12,128,128]{3,2,1,0:T(8,128)(2,1)S(1)}, u32[]{:S(2)}, u32[]{:S(2)}) collective-permute-start(bf16[1,12,128,128]{3,2,1,0:T(8,128)(2,1)} %bitcast.31), channel_id=1, source_target_pairs={{0,2},{1,15},{2,4},{3,1},{4,6},{5,3},{6,8},{7,5},{8,10},{9,7},{10,... | collective-permute-start | bytes 1179656 | tf_op jit(solution)/shard_map/ppermute | solution.py:309
  110.3 1.7 %slice_bitcast_fusion = bf16[2,2,64,24,128]{4,3,0,2,1:T(8,128)(2,1)S(1)} fusion(bf16[2,64,6,24,128]{4,3,2,1,0:T(8,128)(2,1)} %bitcast.5.received_ref), kind=kLoop, calls=%fused_computation.1 | loop fusion | bytes 3145728 | tf_op jit(solution)/shard_map/transpose | solution.py:338
  112.0 1.7 %dynamic-slice_bitcast_fusion = bf16[4,1,64,24,128]{4,3,0,2,1:T(8,128)(2,1)S(1)} fusion(bf16[2,64,6,24,128]{4,3,2,1,0:T(8,128)(2,1)} %bitcast.5.received_ref, s32[]{:T(128)S(6)} %select_n.36), kind=kLoop, calls=%fused_computation | loop fusion | bytes 3145732 | tf_op jit(solution)/shard_map/transpose | solution.py:338
  113.7 0.3 copy.12
  114.0 0.3 copy.11
  114.2 0.1 constant_dynamic-slice_fusion
  114.3 0.1 pad_maximum_fusion
  114.4 0.1 collective-permute-start
  114.5 9.4 %shard_map.66.refs_8_ = f32[2,1,12,8,128,128]{5,4,3,2,1,0:T(8,128)S(1)} custom-call(s32[3072]{0:T(1024)S(1)} %reshape.34.cols_ref, s32[192]{0:T(256)S(1)} %reshape.35.kept_ref, s32[2]{0:T(128)S(1)} %pad_add_fusion.place_ref, s32[24]{0:T(128)S(1)} %fusion.copy_ref, bf16[4,12,128,128]{3,2,1,0:T(8,128)(2,1)S(1)} %bitcast.25, ...), custom_call_target="tpu_custom_call" | custom-call | flops 805306368 | bytes 26214400 | tf_op jit(solution)/shard_map/pallas_call | solution.py:279
  123.9 7.5 %collective-permute-done.2.refs_4_ = bf16[1,12,128,128]{3,2,1,0:T(8,128)(2,1)S(1)} collective-permute-done((bf16[1,12,128,128]{3,2,1,0:T(8,128)(2,1)}, bf16[1,12,128,128]{3,2,1,0:T(8,128)(2,1)S(1)}, u32[]{:S(2)}, u32[]{:S(2)}) %collective-permute-start.2) | collective-permute-done | bytes 393248 | tf_op jit(solution)/shard_map/ppermute | solution.py:309
  131.4 0.1 pad_maximum_fusion.1
  131.5 4.4 %collective-permute-start.6 = (bf16[2,12,128,128]{3,2,1,0:T(8,128)(2,1)S(1)}, bf16[2,12,128,128]{3,2,1,0:T(8,128)(2,1)S(1)}, u32[]{:S(2)}, u32[]{:S(2)}) collective-permute-start(bf16[2,12,128,128]{3,2,1,0:T(8,128)(2,1)S(1)} %pad_maximum_fusion.1), channel_id=1, source_target_pairs={{0,1},{1,0},{2,3},{3,2},{4,5},{5,4},{6,7},{7,6},{8,9},{9,8},{10,11... | collective-permute-start | bytes 2359304 | tf_op jit(solution)/shard_map/ppermute | solution.py:309
  135.9 1.9 %collective-permute-done.6.refs_7_ = bf16[2,12,128,128]{3,2,1,0:T(8,128)(2,1)S(1)} collective-permute-done((bf16[2,12,128,128]{3,2,1,0:T(8,128)(2,1)S(1)}, bf16[2,12,128,128]{3,2,1,0:T(8,128)(2,1)S(1)}, u32[]{:S(2)}, u32[]{:S(2)}) %collective-permute-start.6) | collective-permute-done | bytes 786464 | tf_op jit(solution)/shard_map/ppermute | solution.py:309
  137.8 12.1 %shard_map.67 = bf16[2,1,12,8,128,128]{5,4,3,2,1,0:T(8,128)(2,1)} custom-call(s32[3072]{0:T(1024)S(1)} %reshape.34.cols_ref, s32[192]{0:T(256)S(1)} %reshape.35.kept_ref, s32[2]{0:T(128)S(1)} %pad_add_fusion.place_ref, s32[28]{0:T(128)S(1)} %fusion.1.copy_ref, bf16[4,12,128,128]{3,2,1,0:T(8,128)(2,1)S(1)} %bitcast.26, ...), custom_call_target="tpu_custom_call" | custom-call | flops 805306368 | bytes 26214400 | tf_op jit(solution)/shard_map/pallas_call | solution.py:279
  (19 shorter events, 0.1 us)
Async XLA Ops:
  0.0 12.1 %copy-start.6 = (s32[2,768]{1,0:T(2,128)S(1)}, s32[2,768]{1,0:T(2,128)}, u32[]{:S(2)}) copy-start(s32[2,768]{1,0:T(2,128)} %constant.55.clone) | copy-start | bytes 18436
  0.0 11.6 %copy-start.5 = (s32[2,1,12,8]{2,3,1,0:T(8,128)S(1)}, s32[2,1,12,8]{2,3,1,0:T(8,128)}, u32[]{:S(2)}) copy-start(s32[2,1,12,8]{2,3,1,0:T(8,128)} %param.8) | copy-start | bytes 2308
  0.0 11.7 %copy-start.4 = (s32[16,16,12]{1,0,2:T(8,128)S(1)}, s32[16,16,12]{1,0,2:T(8,128)}, u32[]{:S(2)}) copy-start(s32[16,16,12]{1,0,2:T(8,128)} %param.7) | copy-start | bytes 36868
  0.0 27.7 %all-to-all-start = ((bf16[128,24,128]{2,1,0:T(8,128)(2,1)}), bf16[128,24,128]{2,1,0:T(8,128)(2,1)S(1)}, u32[]{:S(2)}, u32[]{:S(2)}) async-start(bf16[128,24,128]{2,1,0:T(8,128)(2,1)} %bitcast.33), calls=%async_computation | async-start | bytes 1572864 | tf_op jit(solution)/shard_map/all_to_all | solution.py:322
  29.5 2.2 %copy-start = (bf16[128,6,24,128]{3,2,1,0:T(8,128)(2,1)}, bf16[128,6,24,128]{3,2,1,0:T(8,128)(2,1)S(1)}, u32[]{:S(2)}) copy-start(bf16[128,6,24,128]{3,2,1,0:T(8,128)(2,1)S(1)} %shard_map.64) | copy-start | bytes 14155780
  31.7 67.8 %all-to-all-start.1 = ((bf16[128,6,24,128]{3,2,1,0:T(8,128)(2,1)}), bf16[128,6,24,128]{3,2,1,0:T(8,128)(2,1)}, u32[]{:S(2)}, u32[]{:S(2)}) async-start(bf16[128,6,24,128]{3,2,1,0:T(8,128)(2,1)} %copy-done), calls=%async_computation.1 | async-start | bytes 9437184 | tf_op jit(solution)/shard_map/all_to_all | solution.py:334
  102.0 0.9 copy-start.1
  102.0 1.0 copy-start.2
  102.0 1.1 copy-start.3
  103.2 11.2 %collective-permute-start.3 = (bf16[4,12,128,128]{3,2,1,0:T(8,128)(2,1)S(1)}, bf16[4,12,128,128]{3,2,1,0:T(8,128)(2,1)S(1)}, u32[]{:S(2)}, u32[]{:S(2)}) collective-permute-start(bf16[4,12,128,128]{3,2,1,0:T(8,128)(2,1)S(1)} %bitcast.27), channel_id=1, source_target_pairs={{0,1},{1,0},{2,3},{3,2},{4,5},{5,4},{6,7},{7,6},{8,9},{9,8},{10,11... | collective-permute-start | bytes 4718600 | tf_op jit(solution)/shard_map/ppermute | solution.py:309
  103.2 32.8 %collective-permute-start.5 = (bf16[2,12,128,128]{3,2,1,0:T(8,128)(2,1)}, bf16[2,12,128,128]{3,2,1,0:T(8,128)(2,1)S(1)}, u32[]{:S(2)}, u32[]{:S(2)}) collective-permute-start(bf16[2,12,128,128]{3,2,1,0:T(8,128)(2,1)} %bitcast.29), channel_id=1, source_target_pairs={{0,15},{1,2},{2,1},{3,4},{4,3},{5,6},{6,5},{7,8},{8,7},{9,10},{10,... | collective-permute-start | bytes 2359304 | tf_op jit(solution)/shard_map/ppermute | solution.py:309
  103.2 32.8 %collective-permute-start.4 = (bf16[2,12,128,128]{3,2,1,0:T(8,128)(2,1)}, bf16[2,12,128,128]{3,2,1,0:T(8,128)(2,1)S(1)}, u32[]{:S(2)}, u32[]{:S(2)}) collective-permute-start(bf16[2,12,128,128]{3,2,1,0:T(8,128)(2,1)} %bitcast.30), channel_id=1, source_target_pairs={{0,2},{1,15},{2,4},{3,1},{4,6},{5,3},{6,8},{7,5},{8,10},{9,7},{10,... | collective-permute-start | bytes 2359304 | tf_op jit(solution)/shard_map/ppermute | solution.py:309
  108.7 22.8 %collective-permute-start.2 = (bf16[1,12,128,128]{3,2,1,0:T(8,128)(2,1)}, bf16[1,12,128,128]{3,2,1,0:T(8,128)(2,1)S(1)}, u32[]{:S(2)}, u32[]{:S(2)}) collective-permute-start(bf16[1,12,128,128]{3,2,1,0:T(8,128)(2,1)} %bitcast.32), channel_id=1, source_target_pairs={{0,15},{1,2},{2,1},{3,4},{4,3},{5,6},{6,5},{7,8},{8,7},{9,10},{10,... | collective-permute-start | bytes 1179656 | tf_op jit(solution)/shard_map/ppermute | solution.py:309
  108.7 22.8 %collective-permute-start.1 = (bf16[1,12,128,128]{3,2,1,0:T(8,128)(2,1)}, bf16[1,12,128,128]{3,2,1,0:T(8,128)(2,1)S(1)}, u32[]{:S(2)}, u32[]{:S(2)}) collective-permute-start(bf16[1,12,128,128]{3,2,1,0:T(8,128)(2,1)} %bitcast.31), channel_id=1, source_target_pairs={{0,2},{1,15},{2,4},{3,1},{4,6},{5,3},{6,8},{7,5},{8,10},{9,7},{10,... | collective-permute-start | bytes 1179656 | tf_op jit(solution)/shard_map/ppermute | solution.py:309
  114.4 21.5 %collective-permute-start = (bf16[2,12,128,128]{3,2,1,0:T(8,128)(2,1)S(1)}, bf16[2,12,128,128]{3,2,1,0:T(8,128)(2,1)S(1)}, u32[]{:S(2)}, u32[]{:S(2)}) collective-permute-start(bf16[2,12,128,128]{3,2,1,0:T(8,128)(2,1)S(1)} %pad_maximum_fusion), channel_id=1, source_target_pairs={{0,16},{1,17},{2,18},{3,19},{4,20},{5,21},{6,22},{7,23},{8,24},{9,... | collective-permute-start | bytes 2359304 | tf_op jit(solution)/shard_map/ppermute | solution.py:309
  131.5 6.4 %collective-permute-start.6 = (bf16[2,12,128,128]{3,2,1,0:T(8,128)(2,1)S(1)}, bf16[2,12,128,128]{3,2,1,0:T(8,128)(2,1)S(1)}, u32[]{:S(2)}, u32[]{:S(2)}) collective-permute-start(bf16[2,12,128,128]{3,2,1,0:T(8,128)(2,1)S(1)} %pad_maximum_fusion.1), channel_id=1, source_target_pairs={{0,1},{1,0},{2,3},{3,2},{4,5},{5,4},{6,7},{7,6},{8,9},{9,8},{10,11... | collective-permute-start | bytes 2359304 | tf_op jit(solution)/shard_map/ppermute | solution.py:309

commit v4 on v3

--- a/solution.py
+++ b/solution.py
@@ -142,7 +142,7 @@
 
 
 def pick(route, held):
-    group = 16
+    group = 32
     return pl.pallas_call(
         pick_kernel,
         grid_spec=pltpu.PrefetchScalarGridSpec(
@@ -169,7 +169,7 @@
 
 
 def split(received, half):
-    group = 16
+    group = 32
     sizes = (4, 1, 2, 1)
     results = pl.pallas_call(
         split_kernel,

time: 150 us -> 149 us (level)
  no operation moved by 1% of the time
where the time goes in v4:
time: 149 us
  waiting for transfers between devices  85.9 us (58%)
  starting transfers between devices  28.6 us (19%)
  Pallas kernels  24.9 us (17%)
  local copies, waits for them, and re-layouts  9.19 us (6%)
    all_to_all x1, waiting for transfers between devices, on_device(): lax.all_to_all(outgoing, AXES, split_axis=0, concat_axis=0, tiled=True)  62.3 us
    pallas_call x2, Pallas kernels, products(): pl.pallas_call(functools.partial(product_kernel, len(arrays), from_arrays...  21.5 us
    all_to_all x1, waiting for transfers between devices, on_device(): held = lax.all_to_all(spread, AXES, split_axis=0, concat_axis=0, tiled=True)  14.2 us
    ppermute x7, starting transfers between devices, moved(): return lax.ppermute(tiles, AXES, pairs)  11.6 us
    all_to_all x1, starting transfers between devices, on_device(): held = lax.all_to_all(spread, AXES, split_axis=0, concat_axis=0, tiled=True)  11.5 us
    ppermute x7, waiting for transfers between devices, moved(): return lax.ppermute(tiles, AXES, pairs)  9.42 us
    all_to_all x1, starting transfers between devices, on_device(): lax.all_to_all(outgoing, AXES, split_axis=0, concat_axis=0, tiled=True)  5.47 us
    transpose x4, local copies, waits for them, and re-layouts, gathered(): pieces = pieces[:, :, start:start + count].transpose(2, 0, 1, 3, 4)  3.93 us
  transfers between devices with their start and end apart: 9, of which 4 were waited for; matrix products, arithmetic and copies ran while one was open for 4% of the time, Pallas kernels for 6%

profile of v4, /device:TPU:1, one launch (start us, length us, event | category | flops | bytes accessed | tf_op | source)
XLA Modules:
  0.0 149.0 jit_solution(15267578280177103062)
XLA Ops:
  0.0 11.5 %all-to-all-start = ((bf16[128,24,128]{2,1,0:T(8,128)(2,1)}), bf16[128,24,128]{2,1,0:T(8,128)(2,1)S(1)}, u32[]{:S(2)}, u32[]{:S(2)}) async-start(bf16[128,24,128]{2,1,0:T(8,128)(2,1)} %bitcast.33), calls=%async_computation | async-start | bytes 1572864 | tf_op jit(solution)/shard_map/all_to_all | solution.py:322
  11.6 0.1 copy.10
  11.7 0.1 reshape.35.kept_ref
  11.8 0.2 copy.9
  11.9 0.1 reshape.34.cols_ref
  12.1 0.7 fusion.copy_ref
  12.8 0.7 fusion.1.copy_ref
  13.5 0.1 pad_add_fusion.place_ref
  13.6 14.2 %all-to-all-done.held_ref = bf16[128,24,128]{2,1,0:T(8,128)(2,1)S(1)} async-done(((bf16[128,24,128]{2,1,0:T(8,128)(2,1)}), bf16[128,24,128]{2,1,0:T(8,128)(2,1)S(1)}, u32[]{:S(2)}, u32[]{:S(2)}) %all-to-all-start) | async-done | bytes 786464 | tf_op jit(solution)/shard_map/all_to_all | solution.py:322
  27.7 1.7 %shard_map.64 = bf16[128,6,24,128]{3,2,1,0:T(8,128)(2,1)S(1)} custom-call(s32[768]{0:T(1024)S(1)} %dynamic-slice_reduce_fusion.route_ref, bf16[128,24,128]{2,1,0:T(8,128)(2,1)S(1)} %all-to-all-done.held_ref), custom_call_target="tpu_custom_call" | custom-call | bytes 9437184 | tf_op jit(solution)/shard_map/pallas_call | solution.py:146
  29.5 2.2 %copy-done = bf16[128,6,24,128]{3,2,1,0:T(8,128)(2,1)} copy-done((bf16[128,6,24,128]{3,2,1,0:T(8,128)(2,1)}, bf16[128,6,24,128]{3,2,1,0:T(8,128)(2,1)S(1)}, u32[]{:S(2)}) %copy-start) | copy-done | bytes 4718616
  31.6 5.5 %all-to-all-start.1 = ((bf16[128,6,24,128]{3,2,1,0:T(8,128)(2,1)}), bf16[128,6,24,128]{3,2,1,0:T(8,128)(2,1)}, u32[]{:S(2)}, u32[]{:S(2)}) async-start(bf16[128,6,24,128]{3,2,1,0:T(8,128)(2,1)} %copy-done), calls=%async_computation.1 | async-start | bytes 9437184 | tf_op jit(solution)/shard_map/all_to_all | solution.py:334
  37.1 62.3 %all-to-all-done.1 = bf16[128,6,24,128]{3,2,1,0:T(8,128)(2,1)} async-done(((bf16[128,6,24,128]{3,2,1,0:T(8,128)(2,1)}), bf16[128,6,24,128]{3,2,1,0:T(8,128)(2,1)}, u32[]{:S(2)}, u32[]{:S(2)}) %all-to-all-start.1) | async-done | bytes 4718624 | tf_op jit(solution)/shard_map/all_to_all | solution.py:334
  99.4 1.6 %shard_map.65 = (bf16[4,64,24,128]{3,2,1,0:T(8,128)(2,1)S(1)}, bf16[1,64,24,128]{3,2,1,0:T(8,128)(2,1)S(1)}, bf16[2,64,24,128]{3,2,1,0:T(8,128)(2,1)S(1)}, bf16[1,64,24,128]{3,2,1,0:T(8,128)(2,1)S(1)}) custom-call(s32[1]{0:T(128)} %bitcast.10.half_ref, bf16[2,64,6,24,128]{4,3,2,1,0:T(8,128)(2,1)} %bitcast.5.received_ref), custom_call_target="tpu_custom_call" | custom-call | bytes 5242880 | tf_op jit(solution)/shard_map/pallas_call | solution.py:174
  101.1 0.8 copy-done.1
  101.9 0.1 copy-done.2
  102.1 0.2 copy-done.3
  102.2 5.5 %collective-permute-start.4 = (bf16[2,12,128,128]{3,2,1,0:T(8,128)(2,1)}, bf16[2,12,128,128]{3,2,1,0:T(8,128)(2,1)S(1)}, u32[]{:S(2)}, u32[]{:S(2)}) collective-permute-start(bf16[2,12,128,128]{3,2,1,0:T(8,128)(2,1)} %bitcast.30), channel_id=1, source_target_pairs={{0,2},{1,15},{2,4},{3,1},{4,6},{5,3},{6,8},{7,5},{8,10},{9,7},{10,... | collective-permute-start | bytes 2359304 | tf_op jit(solution)/shard_map/ppermute | solution.py:309
  107.7 1.6 %collective-permute-start.1 = (bf16[1,12,128,128]{3,2,1,0:T(8,128)(2,1)}, bf16[1,12,128,128]{3,2,1,0:T(8,128)(2,1)S(1)}, u32[]{:S(2)}, u32[]{:S(2)}) collective-permute-start(bf16[1,12,128,128]{3,2,1,0:T(8,128)(2,1)} %bitcast.31), channel_id=1, source_target_pairs={{0,2},{1,15},{2,4},{3,1},{4,6},{5,3},{6,8},{7,5},{8,10},{9,7},{10,... | collective-permute-start | bytes 1179656 | tf_op jit(solution)/shard_map/ppermute | solution.py:309
  109.3 1.7 %slice_bitcast_fusion = bf16[2,2,64,24,128]{4,3,0,2,1:T(8,128)(2,1)S(1)} fusion(bf16[2,64,6,24,128]{4,3,2,1,0:T(8,128)(2,1)} %bitcast.5.received_ref), kind=kLoop, calls=%fused_computation.1 | loop fusion | bytes 3145728 | tf_op jit(solution)/shard_map/transpose | solution.py:338
  111.0 1.7 %dynamic-slice_bitcast_fusion = bf16[4,1,64,24,128]{4,3,0,2,1:T(8,128)(2,1)S(1)} fusion(bf16[2,64,6,24,128]{4,3,2,1,0:T(8,128)(2,1)} %bitcast.5.received_ref, s32[]{:T(128)S(6)} %select_n.36), kind=kLoop, calls=%fused_computation | loop fusion | bytes 3145732 | tf_op jit(solution)/shard_map/transpose | solution.py:338
  112.7 0.3 copy.12
  113.0 0.3 copy.11
  113.3 0.1 constant_dynamic-slice_fusion
  113.4 0.1 pad_maximum_fusion
  113.5 0.1 collective-permute-start
  113.5 9.4 %shard_map.66.refs_8_ = f32[2,1,12,8,128,128]{5,4,3,2,1,0:T(8,128)S(1)} custom-call(s32[3072]{0:T(1024)S(1)} %reshape.34.cols_ref, s32[192]{0:T(256)S(1)} %reshape.35.kept_ref, s32[2]{0:T(128)S(1)} %pad_add_fusion.place_ref, s32[24]{0:T(128)S(1)} %fusion.copy_ref, bf16[4,12,128,128]{3,2,1,0:T(8,128)(2,1)S(1)} %bitcast.25, ...), custom_call_target="tpu_custom_call" | custom-call | flops 805306368 | bytes 26214400 | tf_op jit(solution)/shard_map/pallas_call | solution.py:279
  123.0 7.5 %collective-permute-done.2.refs_4_ = bf16[1,12,128,128]{3,2,1,0:T(8,128)(2,1)S(1)} collective-permute-done((bf16[1,12,128,128]{3,2,1,0:T(8,128)(2,1)}, bf16[1,12,128,128]{3,2,1,0:T(8,128)(2,1)S(1)}, u32[]{:S(2)}, u32[]{:S(2)}) %collective-permute-start.2) | collective-permute-done | bytes 393248 | tf_op jit(solution)/shard_map/ppermute | solution.py:309
  130.5 0.1 pad_maximum_fusion.1
  130.5 4.4 %collective-permute-start.6 = (bf16[2,12,128,128]{3,2,1,0:T(8,128)(2,1)S(1)}, bf16[2,12,128,128]{3,2,1,0:T(8,128)(2,1)S(1)}, u32[]{:S(2)}, u32[]{:S(2)}) collective-permute-start(bf16[2,12,128,128]{3,2,1,0:T(8,128)(2,1)S(1)} %pad_maximum_fusion.1), channel_id=1, source_target_pairs={{0,1},{1,0},{2,3},{3,2},{4,5},{5,4},{6,7},{7,6},{8,9},{9,8},{10,11... | collective-permute-start | bytes 2359304 | tf_op jit(solution)/shard_map/ppermute | solution.py:309
  135.0 1.9 %collective-permute-done.6.refs_7_ = bf16[2,12,128,128]{3,2,1,0:T(8,128)(2,1)S(1)} collective-permute-done((bf16[2,12,128,128]{3,2,1,0:T(8,128)(2,1)S(1)}, bf16[2,12,128,128]{3,2,1,0:T(8,128)(2,1)S(1)}, u32[]{:S(2)}, u32[]{:S(2)}) %collective-permute-start.6) | collective-permute-done | bytes 786464 | tf_op jit(solution)/shard_map/ppermute | solution.py:309
  136.9 12.1 %shard_map.67 = bf16[2,1,12,8,128,128]{5,4,3,2,1,0:T(8,128)(2,1)} custom-call(s32[3072]{0:T(1024)S(1)} %reshape.34.cols_ref, s32[192]{0:T(256)S(1)} %reshape.35.kept_ref, s32[2]{0:T(128)S(1)} %pad_add_fusion.place_ref, s32[28]{0:T(128)S(1)} %fusion.1.copy_ref, bf16[4,12,128,128]{3,2,1,0:T(8,128)(2,1)S(1)} %bitcast.26, ...), custom_call_target="tpu_custom_call" | custom-call | flops 805306368 | bytes 26214400 | tf_op jit(solution)/shard_map/pallas_call | solution.py:279
  (19 shorter events, 0.1 us)
Async XLA Ops:
  0.0 12.1 %copy-start.6 = (s32[2,768]{1,0:T(2,128)S(1)}, s32[2,768]{1,0:T(2,128)}, u32[]{:S(2)}) copy-start(s32[2,768]{1,0:T(2,128)} %constant.55.clone) | copy-start | bytes 18436
  0.0 11.6 %copy-start.5 = (s32[2,1,12,8]{2,3,1,0:T(8,128)S(1)}, s32[2,1,12,8]{2,3,1,0:T(8,128)}, u32[]{:S(2)}) copy-start(s32[2,1,12,8]{2,3,1,0:T(8,128)} %param.8) | copy-start | bytes 2308
  0.0 11.7 %copy-start.4 = (s32[16,16,12]{1,0,2:T(8,128)S(1)}, s32[16,16,12]{1,0,2:T(8,128)}, u32[]{:S(2)}) copy-start(s32[16,16,12]{1,0,2:T(8,128)} %param.7) | copy-start | bytes 36868
  0.0 27.7 %all-to-all-start = ((bf16[128,24,128]{2,1,0:T(8,128)(2,1)}), bf16[128,24,128]{2,1,0:T(8,128)(2,1)S(1)}, u32[]{:S(2)}, u32[]{:S(2)}) async-start(bf16[128,24,128]{2,1,0:T(8,128)(2,1)} %bitcast.33), calls=%async_computation | async-start | bytes 1572864 | tf_op jit(solution)/shard_map/all_to_all | solution.py:322
  29.4 2.2 %copy-start = (bf16[128,6,24,128]{3,2,1,0:T(8,128)(2,1)}, bf16[128,6,24,128]{3,2,1,0:T(8,128)(2,1)S(1)}, u32[]{:S(2)}) copy-start(bf16[128,6,24,128]{3,2,1,0:T(8,128)(2,1)S(1)} %shard_map.64) | copy-start | bytes 14155780
  31.6 67.8 %all-to-all-start.1 = ((bf16[128,6,24,128]{3,2,1,0:T(8,128)(2,1)}), bf16[128,6,24,128]{3,2,1,0:T(8,128)(2,1)}, u32[]{:S(2)}, u32[]{:S(2)}) async-start(bf16[128,6,24,128]{3,2,1,0:T(8,128)(2,1)} %copy-done), calls=%async_computation.1 | async-start | bytes 9437184 | tf_op jit(solution)/shard_map/all_to_all | solution.py:334
  101.1 0.9 copy-start.1
  101.1 1.0 copy-start.2
  101.1 1.1 copy-start.3
  102.2 11.2 %collective-permute-start.3 = (bf16[4,12,128,128]{3,2,1,0:T(8,128)(2,1)S(1)}, bf16[4,12,128,128]{3,2,1,0:T(8,128)(2,1)S(1)}, u32[]{:S(2)}, u32[]{:S(2)}) collective-permute-start(bf16[4,12,128,128]{3,2,1,0:T(8,128)(2,1)S(1)} %bitcast.27), channel_id=1, source_target_pairs={{0,1},{1,0},{2,3},{3,2},{4,5},{5,4},{6,7},{7,6},{8,9},{9,8},{10,11... | collective-permute-start | bytes 4718600 | tf_op jit(solution)/shard_map/ppermute | solution.py:309
  102.2 32.8 %collective-permute-start.5 = (bf16[2,12,128,128]{3,2,1,0:T(8,128)(2,1)}, bf16[2,12,128,128]{3,2,1,0:T(8,128)(2,1)S(1)}, u32[]{:S(2)}, u32[]{:S(2)}) collective-permute-start(bf16[2,12,128,128]{3,2,1,0:T(8,128)(2,1)} %bitcast.29), channel_id=1, source_target_pairs={{0,15},{1,2},{2,1},{3,4},{4,3},{5,6},{6,5},{7,8},{8,7},{9,10},{10,... | collective-permute-start | bytes 2359304 | tf_op jit(solution)/shard_map/ppermute | solution.py:309
  102.2 32.8 %collective-permute-start.4 = (bf16[2,12,128,128]{3,2,1,0:T(8,128)(2,1)}, bf16[2,12,128,128]{3,2,1,0:T(8,128)(2,1)S(1)}, u32[]{:S(2)}, u32[]{:S(2)}) collective-permute-start(bf16[2,12,128,128]{3,2,1,0:T(8,128)(2,1)} %bitcast.30), channel_id=1, source_target_pairs={{0,2},{1,15},{2,4},{3,1},{4,6},{5,3},{6,8},{7,5},{8,10},{9,7},{10,... | collective-permute-start | bytes 2359304 | tf_op jit(solution)/shard_map/ppermute | solution.py:309
  107.7 22.8 %collective-permute-start.2 = (bf16[1,12,128,128]{3,2,1,0:T(8,128)(2,1)}, bf16[1,12,128,128]{3,2,1,0:T(8,128)(2,1)S(1)}, u32[]{:S(2)}, u32[]{:S(2)}) collective-permute-start(bf16[1,12,128,128]{3,2,1,0:T(8,128)(2,1)} %bitcast.32), channel_id=1, source_target_pairs={{0,15},{1,2},{2,1},{3,4},{4,3},{5,6},{6,5},{7,8},{8,7},{9,10},{10,... | collective-permute-start | bytes 1179656 | tf_op jit(solution)/shard_map/ppermute | solution.py:309
  107.7 22.8 %collective-permute-start.1 = (bf16[1,12,128,128]{3,2,1,0:T(8,128)(2,1)}, bf16[1,12,128,128]{3,2,1,0:T(8,128)(2,1)S(1)}, u32[]{:S(2)}, u32[]{:S(2)}) collective-permute-start(bf16[1,12,128,128]{3,2,1,0:T(8,128)(2,1)} %bitcast.31), channel_id=1, source_target_pairs={{0,2},{1,15},{2,4},{3,1},{4,6},{5,3},{6,8},{7,5},{8,10},{9,7},{10,... | collective-permute-start | bytes 1179656 | tf_op jit(solution)/shard_map/ppermute | solution.py:309
  113.5 21.5 %collective-permute-start = (bf16[2,12,128,128]{3,2,1,0:T(8,128)(2,1)S(1)}, bf16[2,12,128,128]{3,2,1,0:T(8,128)(2,1)S(1)}, u32[]{:S(2)}, u32[]{:S(2)}) collective-permute-start(bf16[2,12,128,128]{3,2,1,0:T(8,128)(2,1)S(1)} %pad_maximum_fusion), channel_id=1, source_target_pairs={{0,16},{1,17},{2,18},{3,19},{4,20},{5,21},{6,22},{7,23},{8,24},{9,... | collective-permute-start | bytes 2359304 | tf_op jit(solution)/shard_map/ppermute | solution.py:309
  130.5 6.4 %collective-permute-start.6 = (bf16[2,12,128,128]{3,2,1,0:T(8,128)(2,1)S(1)}, bf16[2,12,128,128]{3,2,1,0:T(8,128)(2,1)S(1)}, u32[]{:S(2)}, u32[]{:S(2)}) collective-permute-start(bf16[2,12,128,128]{3,2,1,0:T(8,128)(2,1)S(1)} %pad_maximum_fusion.1), channel_id=1, source_target_pairs={{0,1},{1,0},{2,3},{3,2},{4,5},{5,4},{6,7},{7,6},{8,9},{9,8},{10,11... | collective-permute-start | bytes 2359304 | tf_op jit(solution)/shard_map/ppermute | solution.py:309
